TPU v7x, 32 devices: a whole 2x2x4 slice. The times are simulated.
32 devices in a mesh: ctx: 8 (over z, y), wt: 4 (over x, core).
Axes of the slice: x: 2, y: 2, z: 4, core: 2. Of those that a mesh axis runs over, the one named last changes fastest.
Arguments:
- block_in: bfloat16 [4096, 1024], P('ctx'), may hold values from -6 to 6
- doc_ids: int32 [4096], replicated, may hold values from 0 to 3, as said below
- block_of: int32 [16], replicated, may hold values from 0 to 15, as said below
- w_query: bfloat16 [1024, 1024], P(None, 'wt'), may hold values from -0.1875 to 0.1875
- w_key: bfloat16 [1024, 512], P(None, 'wt'), may hold values from -0.1875 to 0.1875
- w_value: bfloat16 [1024, 512], P(None, 'wt'), may hold values from -0.1875 to 0.1875
- w_out: bfloat16 [1024, 1024], P('wt'), may hold values from -1.5 to 1.5
- w_gate: bfloat16 [1024, 4608], P(None, 'wt'), may hold values from -0.1875 to 0.1875
- w_up: bfloat16 [1024, 4608], P(None, 'wt'), may hold values from -0.1875 to 0.1875
- w_down: bfloat16 [4608, 1024], P('wt'), may hold values from -0.09375 to 0.09375
- attn_gain: float32 [1024], replicated, may hold values from 0.5 to 1.5
- ffn_gain: float32 [1024], replicated, may hold values from 0.5 to 1.5
- query_gain: float32 [64], replicated, may hold values from 1 to 2
- key_gain: float32 [64], replicated, may hold values from 0.1 to 1.9
- cotangent: bfloat16 [4096, 1024], P('ctx'), may hold values from -8 to 8
Outputs:
- block_out: bfloat16 [4096, 1024], P('ctx')
- input_grad: float32 [4096, 1024], P('ctx')
- grad_query: float32 [1024, 1024], P('ctx', 'wt')
- grad_key: float32 [1024, 512], P('ctx', 'wt')
- grad_value: float32 [1024, 512], P('ctx', 'wt')
- grad_out_proj: float32 [1024, 1024], P('wt', 'ctx')
- grad_gate: float32 [1024, 4608], P('ctx', 'wt')
- grad_up: float32 [1024, 4608], P('ctx', 'wt')
- grad_down: float32 [4608, 1024], P('wt', 'ctx')
- grad_attn_gain: float32 [1024], P('ctx')
- grad_ffn_gain: float32 [1024], P('ctx')
- grad_query_gain: float32 [64], P('ctx')
- grad_key_gain: float32 [64], P('ctx')
Inputs may be any that keep to these rules, and one draw needn't show every extreme that they name: doc_ids never falls along the text order, is 0 at the first token and 3 at the last, and document 0 holds at least the first 2048 tokens. block_of is a permutation of 0 to 15 whose entries 2c and 2c + 1 sum to 15 for every c.
All inputs are finite; a program needn't handle non-finite values.
Results may differ from a plain program's by a relative error of at most 0.029.
Values may be sent and summed in bfloat16 or wider, within the bound.
No kernel may reach another device: no remote copies, remote signals or barrier semaphores. Data moves between devices by JAX's collectives and lax.ppermute only.
A program may use at most 128 MiB of HBM per device.

v0:
```python
import functools

import jax
import jax.numpy as jnp
import numpy as np
from jax import lax
from jax.experimental import pallas as pl
from jax.experimental.pallas import tpu as pltpu
from jax.sharding import PartitionSpec as P

EPS = 1e-05
THETA = 1000000.0
NEG = -1e30
SCALE = 0.125
LANES = 128
DOCS = 4
FORWARD_ROWS = 512
BACK_ROWS = 512
GAIN_ROWS = 16
VMEM_LIMIT = 60 * 1024 * 1024
F32 = jnp.float32
BF16 = jnp.bfloat16


def matmul(left, right):
    return jnp.dot(left, right, preferred_element_type=F32)


def contract(left, right, left_dim, right_dim):
    return lax.dot_general(
        left, right, (((left_dim,), (right_dim,)), ((), ())), preferred_element_type=F32
    )


def rms_norm(vector, gain):
    return vector * lax.rsqrt(jnp.mean(vector * vector, axis=-1, keepdims=True) + EPS) * gain


def norm_back(vector, gain, gradient):
    inverse = lax.rsqrt(jnp.mean(vector * vector, axis=-1, keepdims=True) + EPS)
    scaled = gradient * gain
    back = inverse * scaled - vector * inverse**3 * jnp.mean(
        scaled * vector, axis=-1, keepdims=True
    )
    return (back, gradient * vector * inverse)


def lane_index(shape):
    return lax.broadcasted_iota(jnp.int32, shape, len(shape) - 1)


def head_mean(values, head_dim):
    row_id = lax.broadcasted_iota(jnp.int32, (LANES, LANES), 0) // head_dim
    col_id = lax.broadcasted_iota(jnp.int32, (LANES, LANES), 1) // head_dim
    ones = (row_id == col_id).astype(BF16)
    high = values.astype(BF16)
    low = (values - high.astype(F32)).astype(BF16)
    return (matmul(high, ones) + matmul(low, ones)) * (1.0 / head_dim)


def swap_halves(values, head_dim):
    half = head_dim // 2
    lane = lane_index(values.shape)
    return jnp.where(
        lane % head_dim < half,
        pltpu.roll(values, LANES - half, 1),
        pltpu.roll(values, half, 1),
    )


def mix_heads(first, second, head_dim):
    lane = lane_index(first.shape)
    return (
        jnp.where(lane < head_dim, first, pltpu.roll(second, head_dim, 1)),
        jnp.where(lane < head_dim, pltpu.roll(first, head_dim, 1), second),
    )


def mix_low(first, second, head_dim):
    one, two = mix_heads(first.astype(F32), second.astype(F32), head_dim)
    return one.astype(BF16), two.astype(BF16)


def block_tables(base_cos, base_sin, step_cos, step_sin, head_dim):
    cos = base_cos * step_cos - base_sin * step_sin
    sin = base_sin * step_cos + base_cos * step_sin
    lane = lane_index(cos.shape)
    return cos, jnp.where(lane % head_dim < head_dim // 2, -sin, sin)


def head_norm_back(raw, gain, gradient, head_dim):
    inverse = lax.rsqrt(head_mean(raw * raw, head_dim) + EPS)
    scaled = gradient * gain
    back = inverse * scaled - raw * inverse**3 * head_mean(scaled * raw, head_dim)
    return back, jnp.sum(gradient * raw * inverse, axis=0, keepdims=True)


class Info:
    def __init__(self, block_ref, start_ref, devices, half_rows):
        self.block_ref, self.start_ref = block_ref, start_ref
        self.devices, self.half_rows = devices, half_rows
        self.ctx, self.core = lax.axis_index("ctx"), lax.rem(lax.axis_index("wt"), 2)

    def block(self, source, half):
        return self.block_ref[2 * source + jnp.bitwise_xor(half, self.core)]

    def slot_source(self, slot):
        pairs = self.devices // 2
        same = slot < pairs
        column = jnp.where(same, self.ctx, jnp.bitwise_xor(self.ctx, 1))
        step = jnp.where(same, slot, slot - pairs)
        return lax.rem(column - 2 * step + self.devices, self.devices)

    def doc_start(self, position):
        start = jnp.zeros_like(position)
        for doc in range(1, DOCS):
            first = self.start_ref[doc]
            start = jnp.where(position >= first, first, start)
        return start

    def relation(self, query_block, key_block):
        rows = self.half_rows
        low = self.doc_start(query_block * rows)
        high = self.doc_start(query_block * rows + rows - 1)
        visible = (key_block <= query_block) & (key_block * rows + rows - 1 >= low)
        whole = (key_block < query_block) & (key_block * rows >= high)
        return visible, whole

    def mask(self, query_block, key_block, query_dim):
        rows = self.half_rows
        query_pos = query_block * rows + lax.broadcasted_iota(jnp.int32, (rows, rows), query_dim)
        key_pos = key_block * rows + lax.broadcasted_iota(jnp.int32, (rows, rows), 1 - query_dim)
        return (key_pos <= query_pos) & (key_pos >= self.doc_start(query_pos))


def rope_rows(info, tables, half, head_dim):
    base_cos, base_sin, step_cos, step_sin = tables
    block = info.block(info.ctx, half)
    return block_tables(
        base_cos[pl.ds(block, 1), :],
        base_sin[pl.ds(block, 1), :],
        step_cos[...],
        step_sin[...],
        head_dim,
    )


def half_slice(half, rows):
    return slice(half * rows, half * rows + rows)


def twice(ref):
    row = ref[...]
    return jnp.concatenate([row] * (LANES // row.shape[1]), axis=1)


def project_kernel(devices, head_dim, block_ref, x_ref, doc_ref, gain_ref, wq_ref, wk_ref, wv_ref,
                   qg_ref, kg_ref, bc_ref, bs_ref, sc_ref, ss_ref,
                   kv_ref, q_ref, raw_ref, n1_ref, x_out, start_ref):
    rows = x_ref.shape[0] // 2
    start_ref[0] = 0
    for doc in range(1, DOCS):
        start_ref[doc] = jnp.sum((doc_ref[...] < doc).astype(jnp.int32))
    info = Info(block_ref, start_ref, devices, rows)
    tables = (bc_ref, bs_ref, sc_ref, ss_ref)
    query_gain, key_gain = twice(qg_ref), twice(kg_ref)
    chunks = wq_ref.shape[1] // LANES
    for half in range(2):
        here = half_slice(half, rows)
        from_row = pl.multiple_of(jnp.bitwise_xor(half, info.core) * rows, rows)
        x_low = x_ref[pl.ds(from_row, rows), :]
        x_out[here, :] = x_low
        normed = rms_norm(x_low.astype(F32), gain_ref[...]).astype(BF16)
        n1_ref[here, :] = normed
        cos, sin = rope_rows(info, tables, half, head_dim)

        def turned(raw, gain):
            unit = raw * lax.rsqrt(head_mean(raw * raw, head_dim) + EPS) * gain
            return unit * cos + swap_halves(unit, head_dim) * sin

        key_raw = matmul(normed, wk_ref[...])
        kv_ref[here, 0:LANES] = turned(key_raw, key_gain).astype(BF16)
        kv_ref[here, LANES : 2 * LANES] = matmul(normed, wv_ref[...]).astype(BF16)
        raw_ref[here, chunks * LANES : (chunks + 1) * LANES] = key_raw
        query_raw = matmul(normed, wq_ref[...])
        raw_ref[here, 0 : chunks * LANES] = query_raw
        for chunk in range(chunks):
            cols = slice(chunk * LANES, (chunk + 1) * LANES)
            q_ref[here, cols] = (turned(query_raw[:, cols], query_gain) * SCALE).astype(BF16)


def spread_heads(low, rows, half, head_dim, out_ref):
    here = half_slice(half, rows)
    groups = mix_low(low[here, 0:LANES], low[here, LANES : 2 * LANES], head_dim)
    lane = lane_index((rows, LANES))
    for kv in range(2):
        for group in range(2):
            at = (2 * kv + group) * rows
            out_ref[half, at : at + rows, :] = jnp.where(
                lane // head_dim == kv, groups[group].astype(F32), 0.0
            ).astype(BF16)


def join_heads(stacked, rows, head_dim):
    lane = lane_index((rows, LANES))
    groups = [
        jnp.where(
            lane < head_dim,
            stacked[group * rows : (group + 1) * rows],
            stacked[(2 + group) * rows : (3 + group) * rows],
        )
        for group in range(2)
    ]
    return mix_heads(groups[0], groups[1], head_dim)


def fetch(pairs_of_refs, sems):
    copies = [
        pltpu.make_async_copy(source, target, sems.at[at])
        for at, (source, target) in enumerate(pairs_of_refs)
    ]
    for copy in copies:
        copy.start()
    return copies


def attend_slots(info, first_slot, held, spread, total):
    rows = info.half_rows

    def one_key_block(step, carry):
        slot, key_half = step // 2, lax.rem(step, 2)
        key_block = info.block(info.slot_source(first_slot + slot), key_half)
        key_rows = pl.ds(pl.multiple_of(key_half * rows, rows), rows)
        for half in range(2):
            query_block = info.block(info.ctx, half)
            visible, whole = info.relation(query_block, key_block)

            def take(masked, half=half, query_block=query_block):
                keys = held[slot, key_rows, 0:LANES]
                values = jnp.concatenate(
                    [held[slot, key_rows, LANES : 2 * LANES], jnp.ones((rows, LANES), BF16)], axis=1
                )
                if masked:
                    allowed = info.mask(query_block, key_block, 0)
                    allowed = jnp.concatenate([allowed] * (FORWARD_ROWS // rows), axis=0)
                for part in range(4 * rows // FORWARD_ROWS):
                    at = slice(part * FORWARD_ROWS, (part + 1) * FORWARD_ROWS)
                    scores = contract(spread[half, at, :], keys, 1, 1)
                    if masked:
                        scores = jnp.where(allowed, scores, NEG)
                    weights = jnp.exp(scores).astype(BF16)
                    total[half, at, :] += matmul(weights, values)

            pl.when(visible & whole)(functools.partial(take, False))
            pl.when(visible & jnp.logical_not(whole))(functools.partial(take, True))
        return carry

    lax.fori_loop(0, 2 * held.shape[0], one_key_block, 0)


def attend_first_kernel(devices, head_dim, block_ref, start_ref, q_ref, *refs):
    count = devices // 2 + 1
    slots = refs[:count]
    total, spread, held, sems = refs[count:]
    rows = q_ref.shape[0] // 2
    info = Info(block_ref, start_ref, devices, rows)
    copies = fetch([(slots[at], held.at[at]) for at in range(count)], sems)
    q_low = q_ref[...]
    for half in range(2):
        spread_heads(q_low, rows, half, head_dim, spread)
    total[...] = jnp.zeros_like(total)
    for copy in copies:
        copy.wait()
    attend_slots(info, 0, held, spread, total)


def attend_second_kernel(devices, head_dim, block_ref, start_ref, spread, total_ref, wo_ref, *refs):
    count = devices // 2 - 1
    slots = refs[:count]
    o_ref, o32_ref, lse_ref, mine_ref, other_ref, held, total, sems = refs[count:]
    rows = o_ref.shape[0] // 2
    info = Info(block_ref, start_ref, devices, rows)
    copies = fetch(
        [(slots[at], held.at[at]) for at in range(count)] + [(total_ref, total)], sems
    )
    for copy in copies:
        copy.wait()
    attend_slots(info, devices - count, held, spread, total)
    for half in (1, 0):
        here = half_slice(half, rows)
        sums = total[half, :, LANES : 2 * LANES]
        chunks = join_heads(total[half, :, 0:LANES] / sums, rows, head_dim)
        for chunk in range(2):
            cols = slice(chunk * LANES, (chunk + 1) * LANES)
            o32_ref[here, cols] = chunks[chunk]
            o_ref[here, cols] = chunks[chunk].astype(BF16)
        lse_ref[half] = jnp.transpose(jnp.log(sums))[0:8, :]
        part = matmul(o_ref[here, :], wo_ref[...]).astype(BF16)
        (mine_ref, other_ref)[half][...] = part


def feed_kernel(x_ref, mine_ref, other_ref, gain_ref, wg_ref, wu_ref, dh_ref,
                mid_ref, n2_ref, hid_ref, dgate_ref, dup_ref, part_mine, part_other):
    rows = x_ref.shape[0] // 2
    hidden = wg_ref.shape[1]
    for half in range(2):
        here = half_slice(half, rows)
        middle = x_ref[here, :].astype(F32) + (mine_ref, other_ref)[half][...].astype(F32)
        mid_ref[here, :] = middle
        n2_ref[here, :] = rms_norm(middle, gain_ref[...]).astype(BF16)
    step = 2 * LANES
    for at in range(0, hidden, step):
        cols = slice(at, min(at + step, hidden))
        normed = n2_ref[...]
        gate = matmul(normed, wg_ref[:, cols])
        up = matmul(normed, wu_ref[:, cols])
        grad_hidden = dh_ref[:, cols]
        sigmoid = jax.nn.sigmoid(gate)
        silu = gate * sigmoid
        hid_ref[:, cols] = (silu * up).astype(BF16)
        dgate_ref[:, cols] = (
            grad_hidden * up * sigmoid * (1.0 + gate * (1.0 - sigmoid))
        ).astype(BF16)
        dup_ref[:, cols] = (grad_hidden * silu).astype(BF16)
    for half, part in ((1, part_other), (0, part_mine)):
        here = half_slice(half, rows)
        for at in range(0, wg_ref.shape[0], step):
            wide = slice(at, at + step)
            part[:, wide] = (
                contract(dgate_ref[here, :], wg_ref[wide, :], 1, 1)
                + contract(dup_ref[here, :], wu_ref[wide, :], 1, 1)
            ).astype(BF16)


def prepare_back(info, head_dim, q_ref, do_ref, o32_ref, spread, spread_do, delta):
    rows = info.half_rows
    q_low, do_low = q_ref[...], do_ref[...]
    for half in range(2):
        here = half_slice(half, rows)
        spread_heads(q_low, rows, half, head_dim, spread)
        spread_heads(do_low, rows, half, head_dim, spread_do)
        product = do_low[here, :].astype(F32) * o32_ref[here, :]
        for chunk in range(2):
            turned = jnp.transpose(product[:, chunk * LANES : (chunk + 1) * LANES])
            for group in range(2):
                at = (2 * chunk + group) * rows
                delta[half, :, at : at + rows] = jnp.broadcast_to(
                    jnp.sum(
                        turned[group * head_dim : (group + 1) * head_dim], axis=0, keepdims=True
                    ),
                    (8, rows),
                )


def back_slots(info, first_slot, held, spread, spread_do, lse_ref, delta, dq_t, dkv, out_ref):
    rows = info.half_rows

    def one_key_block(step, carry):
        slot, key_half = step // 2, lax.rem(step, 2)
        source = info.slot_source(first_slot + slot)
        key_block = info.block(source, key_half)
        key_rows = pl.ds(pl.multiple_of(key_half * rows, rows), rows)
        dkv[...] = jnp.zeros_like(dkv)
        for half in range(2):
            query_block = info.block(info.ctx, half)
            visible, whole = info.relation(query_block, key_block)

            def take(masked, half=half, query_block=query_block):
                keys = held[slot, key_rows, 0:LANES]
                values = held[slot, key_rows, LANES : 2 * LANES]
                if masked:
                    allowed = info.mask(query_block, key_block, 1)
                    allowed = jnp.concatenate([allowed] * (BACK_ROWS // rows), axis=1)
                for part in range(4 * rows // BACK_ROWS):
                    at = slice(part * BACK_ROWS, (part + 1) * BACK_ROWS)
                    queries, grads = spread[half, at, :], spread_do[half, at, :]
                    scores = contract(keys, queries, 1, 1) - lse_ref[half, 0:1, at]
                    if masked:
                        scores = jnp.where(allowed, scores, NEG)
                    probs = jnp.exp(scores)
                    grad_probs = contract(values, grads, 1, 1)
                    grad_scores = (probs * (grad_probs - delta[half, 0:1, at])).astype(BF16)
                    dkv[:, LANES : 2 * LANES] += matmul(probs.astype(BF16), grads)
                    dkv[:, 0:LANES] += matmul(grad_scores, queries)
                    dq_t[half, :, at] += contract(keys, grad_scores, 0, 0)

            pl.when(visible & whole)(functools.partial(take, False))
            pl.when(visible & jnp.logical_not(whole))(functools.partial(take, True))
        out_ref[source // 2, key_rows, :] = dkv[...].astype(BF16)
        return carry

    lax.fori_loop(0, 2 * held.shape[0], one_key_block, 0)


def back_first_kernel(devices, head_dim, wt_count, block_ref, start_ref, q_ref, o32_ref, lse_ref,
                      mid_ref, mine_ref, other_ref, c_ref, gain_ref, wo_ref, *refs):
    pairs = devices // 2
    slots = refs[:pairs]
    dkv_out, dq_t, dy_ref, dyb_ref, do_ref, ffn_gain = refs[pairs : pairs + 6]
    held, spread, spread_do, delta, dkv, sems = refs[pairs + 6 :]
    rows = q_ref.shape[0] // 2
    info = Info(block_ref, start_ref, devices, rows)
    copies = fetch([(slots[at], held.at[at]) for at in range(pairs)], sems)
    gain_sum = jnp.zeros((1, gain_ref.shape[1]), F32)
    for half in range(2):
        here = half_slice(half, rows)
        back, terms = norm_back(
            mid_ref[here, :], gain_ref[...], (mine_ref, other_ref)[half][...].astype(F32)
        )
        gain_sum += jnp.sum(terms, axis=0, keepdims=True)
        grad_middle = c_ref[here, :].astype(F32) + back
        dy_ref[here, :] = grad_middle
        dyb_ref[here, :] = grad_middle.astype(BF16)
        do_ref[here, :] = contract(dyb_ref[here, :], wo_ref[...], 1, 1).astype(BF16)
    ffn_gain[...] = gain_sum * (1.0 / wt_count)
    prepare_back(info, head_dim, q_ref, do_ref, o32_ref, spread, spread_do, delta)
    dq_t[...] = jnp.zeros_like(dq_t)
    for copy in copies:
        copy.wait()
    back_slots(info, pairs, held, spread, spread_do, lse_ref, delta, dq_t, dkv, dkv_out)


def back_second_kernel(devices, head_dim, block_ref, start_ref, q_ref, do_ref, o32_ref, lse_ref,
                       raw_ref, qg_ref, bc_ref, bs_ref, sc_ref, ss_ref, dq_in, *refs):
    pairs = devices // 2
    slots = refs[:pairs]
    dkv_out, dq_ref, gain_ref, held, spread, spread_do, delta, dq_t, dkv, sems = refs[pairs:]
    rows = q_ref.shape[0] // 2
    info = Info(block_ref, start_ref, devices, rows)
    copies = fetch([(slots[at], held.at[at]) for at in range(pairs)] + [(dq_in, dq_t)], sems)
    prepare_back(info, head_dim, q_ref, do_ref, o32_ref, spread, spread_do, delta)
    for copy in copies:
        copy.wait()
    back_slots(info, 0, held, spread, spread_do, lse_ref, delta, dq_t, dkv, dkv_out)
    query_gain = twice(qg_ref)
    gain_sum = jnp.zeros((1, LANES), F32)
    for half in range(2):
        here = half_slice(half, rows)
        cos, sin = rope_rows(info, (bc_ref, bs_ref, sc_ref, ss_ref), half, head_dim)
        chunks = join_heads(jnp.transpose(dq_t[half]), rows, head_dim)
        for chunk in range(2):
            cols = slice(chunk * LANES, (chunk + 1) * LANES)
            grad = chunks[chunk] * SCALE
            grad = grad * cos - swap_halves(grad, head_dim) * sin
            back, term = head_norm_back(raw_ref[here, cols], query_gain, grad, head_dim)
            dq_ref[here, cols] = back.astype(BF16)
            gain_sum += term
    gain_ref[...] = gain_sum


def key_back_kernel(devices, head_dim, count, block_ref, start_ref, raw_ref, kg_ref, bc_ref, bs_ref,
                    sc_ref, ss_ref, dq_ref, x_ref, wq_ref, wk_ref, wv_ref, ffn_gain, query_gain,
                    *refs):
    parts = refs[:count]
    dkv_ref, mine_ref, other_ref, gains_ref = refs[count:]
    rows = raw_ref.shape[0] // 2
    width = x_ref.shape[1]
    info = Info(block_ref, start_ref, devices, rows)
    key_gain = twice(kg_ref)
    key_sum = jnp.zeros((1, LANES), F32)
    attn_sum = jnp.zeros((1, width), F32)
    for half in (1, 0):
        here = half_slice(half, rows)
        grad = sum(part[here, :].astype(F32) for part in parts)
        cos, sin = rope_rows(info, (bc_ref, bs_ref, sc_ref, ss_ref), half, head_dim)
        grad_k = grad[:, 0:LANES]
        grad_k = grad_k * cos - swap_halves(grad_k, head_dim) * sin
        back, term = head_norm_back(raw_ref[here, 2 * LANES : 3 * LANES], key_gain, grad_k, head_dim)
        key_sum += term
        key_low, value_low = back.astype(BF16), grad[:, LANES : 2 * LANES].astype(BF16)
        dkv_ref[here, 0:LANES] = key_low
        dkv_ref[here, LANES : 2 * LANES] = value_low
        part = (
            contract(dq_ref[here, :], wq_ref[...], 1, 1)
            + contract(key_low, wk_ref[...], 1, 1)
            + contract(value_low, wv_ref[...], 1, 1)
        )
        (mine_ref, other_ref)[half][...] = part.astype(BF16)
        inputs = x_ref[here, :].astype(F32)
        inverse = lax.rsqrt(jnp.mean(inputs * inputs, axis=-1, keepdims=True) + EPS)
        attn_sum += jnp.sum(part * inputs * inverse, axis=0, keepdims=True)
    gains_ref[:, 0:width] = attn_sum
    gains_ref[:, width : 2 * width] = ffn_gain[...]
    gains_ref[:, 2 * width : 2 * width + LANES] = query_gain[...]
    gains_ref[:, 2 * width + LANES : 2 * width + 2 * LANES] = key_sum


def finish_kernel(x_ref, mine_ref, other_ref, gain_ref, dy_ref, out_ref):
    rows = x_ref.shape[0] // 2
    core = lax.rem(lax.axis_index("wt"), 2)
    for half in range(2):
        here = half_slice(half, rows)
        back, _ = norm_back(
            x_ref[here, :].astype(F32), gain_ref[...], (mine_ref, other_ref)[half][...].astype(F32)
        )
        to_row = pl.multiple_of(jnp.bitwise_xor(half, core) * rows, rows)
        out_ref[pl.ds(to_row, rows), :] = dy_ref[here, :] + back


def put_shard(kept, sent, bit, device, rows, cols, piece):
    index = device // (2 << bit) * (1 << bit) + device % (1 << bit)
    same = lax.rem(lax.axis_index("ctx") // (1 << bit), 2) == device // (1 << bit) % 2

    @pl.when(same)
    def _():
        kept[index, rows, cols] = piece

    @pl.when(jnp.logical_not(same))
    def _():
        sent[index, rows, cols] = piece


def put_rows(kept, sent, bit, shard, row, cols, block):
    for part in range(block.shape[0] // shard):
        piece = block[part * shard : (part + 1) * shard]
        put_shard(kept, sent, bit, row // shard + part, slice(0, shard), cols, piece)


def feed_grad_kernel(per_step, c_ref, n2_ref, hid_ref, dgate_ref, dup_ref, wd_ref, *refs):
    mine_ref, other_ref, y_kept, y_sent, z_kept, z_sent = refs[-6:]
    rows = c_ref.shape[0] // 2
    hidden = hid_ref.shape[1]
    shard, first = y_kept.shape[1:]
    gate_end = z_kept.shape[2]
    gate_at = 2 * hidden - first
    begin = pl.program_id(0) * per_step
    ctx = lax.axis_index("ctx")

    def put(kept, sent, bit, cols, block):
        for part in range(per_step):
            index = part // (2 << bit) * (1 << bit) + part % (1 << bit)
            side = lax.rem((begin + part) // (1 << bit), 2)
            same = lax.rem(ctx // (1 << bit), 2) == side
            piece = block[part * shard : (part + 1) * shard]

            @pl.when(same)
            def _():
                kept[index, :, cols] = piece

            @pl.when(jnp.logical_not(same))
            def _():
                sent[index, :, cols] = piece

    for half, out in ((1, other_ref), (0, mine_ref)):
        out[...] = matmul(hid_ref[half_slice(half, rows), :], wd_ref[...]).astype(BF16)
    turned = jnp.transpose(n2_ref[...])
    block = matmul(turned, dup_ref[...]).astype(BF16)
    put(y_kept, y_sent, 0, slice(0, first), block[:, :first])
    put(z_kept, z_sent, 1, slice(hidden, gate_at), block[:, first:])
    block = matmul(turned, dgate_ref[:, : gate_end - gate_at]).astype(BF16)
    put(z_kept, z_sent, 1, slice(gate_at, gate_end), block)
    block = matmul(jnp.transpose(c_ref[...]), hid_ref[...]).astype(BF16)
    put(z_kept, z_sent, 1, slice(0, hidden), block)


def feed_grads(out_grad, normed, hidden, grad_gate, grad_up, w_down, y_width, z_width, after):
    tok_rows, width = out_grad.shape
    devices = lax.axis_size("ctx")
    shard = width // devices
    step = 2 * LANES
    per_step = step // shard
    pairs = devices // 2
    whole = pl.BlockSpec(hidden.shape, lambda i: (0, 0))
    columns = pl.BlockSpec((tok_rows, step), lambda i: (0, i))
    out = pl.BlockSpec((tok_rows // 2, step), lambda i: (0, i))
    y_spec = pl.BlockSpec((per_step // 2, shard, y_width), lambda i: (i, 0, 0))
    if per_step == 2:
        z_spec = pl.BlockSpec((2, shard, z_width), lambda i: (i // 2, 0, 0))
    else:
        z_spec = pl.BlockSpec((per_step // 2, shard, z_width), lambda i: (i, 0, 0))
    half_low = jax.ShapeDtypeStruct((tok_rows // 2, width), BF16)
    y_shape = jax.ShapeDtypeStruct((pairs, shard, y_width), BF16)
    z_shape = jax.ShapeDtypeStruct((pairs, shard, z_width), BF16)
    return pl.pallas_call(
        functools.partial(feed_grad_kernel, per_step),
        grid=(width // step,),
        out_shape=[half_low, half_low, y_shape, y_shape, z_shape, z_shape],
        in_specs=[columns, columns, whole, whole, whole]
        + [pl.BlockSpec((w_down.shape[0], step), lambda i: (0, i))]
        + [pl.BlockSpec(memory_space=pl.ANY)] * len(after),
        out_specs=[out, out, y_spec, y_spec, z_spec, z_spec],
        compiler_params=pltpu.CompilerParams(vmem_limit_bytes=VMEM_LIMIT),
        cost_estimate=pl.CostEstimate(flops=14 * 10**9, bytes_accessed=0, transcendentals=0),
    )(out_grad, normed, hidden, grad_gate, grad_up, w_down, *after)


def narrow_grad_kernel(devices, skips, *refs):
    kept, sent = refs[-2:]
    count = len(skips)
    width = refs[0].shape[1]
    shard = width // devices
    begin = 0
    if len(refs) > 2 * count + 2:
        gains = refs[2 * count][...]
        for device in range(devices):
            at = device * shard
            blank = [jnp.zeros((1, LANES - shard), F32)] if shard < LANES else []
            first = [gains[:, at : at + shard]] + blank
            second = [gains[:, width + at : width + at + shard]] + blank
            block = jnp.concatenate(
                [
                    jnp.concatenate(first + second, axis=1),
                    gains[:, 2 * width : 2 * width + 2 * LANES],
                    jnp.zeros((GAIN_ROWS - 2, 2 * LANES), F32),
                ],
                axis=0,
            ).astype(BF16)
            put_shard(
                kept, sent, 0, device, slice(shard, shard + GAIN_ROWS), slice(0, 2 * LANES), block
            )
    step = 2 * LANES
    for at in range(count):
        left, right = refs[2 * at], refs[2 * at + 1]
        cols = slice(begin, begin + right.shape[1] - skips[at])
        begin = cols.stop
        for row in range(0, width, step):
            block = matmul(jnp.transpose(left[:, row : row + step]), right[:, skips[at] :])
            block = block.astype(BF16)
            put_rows(kept, sent, 0, shard, row, cols, block)


def call_kernel(body, outs, operands, memory, scratch=(), flops=1000, after=()):
    kinds = {
        "s": pl.BlockSpec(memory_space=pltpu.SMEM),
        "v": pl.BlockSpec(memory_space=pltpu.VMEM),
        "a": pl.BlockSpec(memory_space=pl.ANY),
    }
    count = len(operands)

    def whole(*refs):
        body(*refs[:count], *refs[count + len(after) :])

    return pl.pallas_call(
        whole,
        out_shape=[jax.ShapeDtypeStruct(shape, kind) for shape, kind, *_ in outs],
        in_specs=[kinds[m] for m in memory] + [kinds["a"]] * len(after),
        out_specs=[kinds[out[2] if len(out) > 2 else "v"] for out in outs],
        scratch_shapes=list(scratch),
        compiler_params=pltpu.CompilerParams(vmem_limit_bytes=VMEM_LIMIT),
        cost_estimate=pl.CostEstimate(flops=flops, bytes_accessed=0, transcendentals=0),
    )(*operands, *after)


def hold(values, after):
    return pl.pallas_call(
        lambda *refs: None,
        out_shape=jax.ShapeDtypeStruct(values.shape, values.dtype),
        in_specs=[pl.BlockSpec(memory_space=pl.ANY)] * (1 + len(after)),
        out_specs=pl.BlockSpec(memory_space=pl.ANY),
        input_output_aliases={0: 0},
        cost_estimate=pl.CostEstimate(flops=0, bytes_accessed=0, transcendentals=0),
    )(values, *after)


def flip(values, axis, bit):
    size = lax.axis_size(axis)
    return lax.ppermute(values, axis, [(i, i ^ bit) for i in range(size)])


def shift(values, step):
    size = lax.axis_size("ctx")
    return lax.ppermute(values, "ctx", [(i, (i + step) % size) for i in range(size)])


def gather_slots(values):
    pairs = lax.axis_size("ctx") // 2
    same = [values] + [shift(values, 2 * k) for k in range(1, pairs)]
    return same, [flip(part, "ctx", 1) for part in same]


def chip_sum(mine, other):
    return (mine.astype(F32) + flip(other, "wt", 1).astype(F32)).astype(BF16)


def slice_sum(chip):
    whole = (chip.astype(F32) + flip(chip, "wt", 2).astype(F32)).astype(BF16)
    return whole, flip(whole, "wt", 1)


def halve(kept, received, bits, bit):
    after = len([b for b in bits if b < bit])
    view = (-1, 2, 1 << after) + kept.shape[1:]
    kept, received = kept.reshape(view), received.reshape(view)
    side = (lax.axis_index("ctx") // (1 << bit)) % 2

    def pick(at):
        picked = lax.dynamic_index_in_dim(kept, at, 1, keepdims=False).astype(
            F32
        ) + lax.dynamic_index_in_dim(received, at, 1, keepdims=False).astype(F32)
        return picked.astype(BF16).reshape((-1,) + view[3:])

    return pick(side), pick(1 - side)


def last_sum(kept, received):
    return kept[0].astype(F32) + received[0].astype(F32)


def ctx_bits():
    return range(lax.axis_size("ctx").bit_length() - 1)


def scatter_tail(kept, received, bits):
    bits = list(bits)
    sends = []
    for bit in list(bits):
        kept, sent = halve(kept, received, bits, bit)
        bits.remove(bit)
        sends.append(sent)
        received = flip(sent, "ctx", 1 << bit)
    return last_sum(kept, received), sends


def scatter_tail_from(kept, received, bits):
    if len(bits) == 1:
        return last_sum(kept, received), []
    return scatter_tail(kept, received, bits[1:])


def scatter_rest(kept, received, first, waits=()):
    bits = [bit for bit in ctx_bits() if bit != first]
    sends = []
    for step, bit in enumerate(list(bits)):
        if step < len(waits):
            kept = hold(kept, waits[step])
        kept, sent = halve(kept, received, bits, bit)
        bits.remove(bit)
        sends.append(sent)
        received = flip(sent, "ctx", 1 << bit)
    return last_sum(kept, received), sends


def on_device(
    block_in,
    doc_ids,
    block_of,
    w_query,
    w_key,
    w_value,
    w_out,
    w_gate,
    w_up,
    w_down,
    attn_gain,
    ffn_gain,
    query_gain,
    key_gain,
    cotangent,
):
    tok_rows, width = block_in.shape
    half_rows = tok_rows // 2
    head_dim = query_gain.shape[0]
    q_width, kv_width = w_query.shape[1], w_key.shape[1]
    hidden_width = w_gate.shape[1]
    devices = lax.axis_size("ctx")
    pairs = devices // 2
    blocks = block_of.shape[0]
    wt_count = lax.axis_size("wt")
    ctx = lax.axis_index("ctx")
    core = lax.axis_index("wt") % 2
    mine, other = slice(0, half_rows), slice(half_rows, tok_rows)

    half_dim = head_dim // 2
    freqs = THETA ** (-2.0 * (np.arange(LANES) % half_dim).astype(np.float64) / head_dim)
    base_angle = (np.arange(blocks) * half_rows)[:, None] * freqs[None, :]
    step_angle = np.arange(half_rows)[:, None] * freqs[None, :]
    tables = [
        jnp.asarray(table.astype(np.float32))
        for table in (np.cos(base_angle), np.sin(base_angle), np.cos(step_angle), np.sin(step_angle))
    ]
    attn_gain_row, ffn_gain_row = attn_gain[None, :], ffn_gain[None, :]
    query_gain_row, key_gain_row = query_gain[None, :], key_gain[None, :]
    stacked = 4 * half_rows
    half_low = ((half_rows, width), BF16)
    held = pltpu.VMEM((pairs, tok_rows, 2 * kv_width), BF16)
    spread = pltpu.VMEM((2, stacked, LANES), BF16)

    key_value, query, raw, normed_one, x_local, starts = call_kernel(
        functools.partial(project_kernel, devices, head_dim),
        [
            ((tok_rows, 2 * kv_width), BF16),
            ((tok_rows, q_width), BF16),
            ((tok_rows, q_width + kv_width), F32),
            ((tok_rows, width), BF16),
            ((tok_rows, width), BF16),
            ((DOCS,), jnp.int32, "s"),
        ],
        [
            block_of,
            block_in,
            doc_ids.reshape(-1, LANES),
            attn_gain_row,
            w_query,
            w_key,
            w_value,
            query_gain_row,
            key_gain_row,
        ]
        + tables,
        "s" + "v" * 12,
    )
    place = [block_of, starts]
    same_slots, other_slots = gather_slots(key_value)

    out_grad = jnp.where(core == 0, cotangent, jnp.roll(cotangent, half_rows, 0))
    grad_hidden = contract(out_grad, w_down, 1, 1)

    total, spread_query = call_kernel(
        functools.partial(attend_first_kernel, devices, head_dim),
        [((2, stacked, 2 * LANES), F32), ((2, stacked, LANES), BF16)],
        place + [query] + same_slots + other_slots[:1],
        "ssv" + "a" * (pairs + 1),
        [
            pltpu.VMEM((pairs + 1, tok_rows, 2 * kv_width), BF16),
            pltpu.SemaphoreType.DMA((pairs + 1,)),
        ],
        after=[grad_hidden],
    )
    out_low, out_wide, log_total, attn_mine, attn_other = call_kernel(
        functools.partial(attend_second_kernel, devices, head_dim),
        [
            ((tok_rows, q_width), BF16),
            ((tok_rows, q_width), F32),
            ((2, 8, stacked), F32),
            half_low,
            half_low,
        ],
        place + [spread_query, total, w_out] + other_slots[1:],
        "ssvav" + "a" * (pairs - 1),
        [
            pltpu.VMEM((pairs - 1, tok_rows, 2 * kv_width), BF16),
            pltpu.VMEM((2, stacked, 2 * LANES), F32),
            pltpu.SemaphoreType.DMA((pairs,)),
        ],
    )
    attn_mine, attn_other = slice_sum(chip_sum(attn_mine, attn_other))

    middle, normed_two, hidden, grad_gate, grad_upper, part_mine, part_other = call_kernel(
        feed_kernel,
        [
            ((tok_rows, width), F32),
            ((tok_rows, width), BF16),
            ((tok_rows, hidden_width), BF16),
            ((tok_rows, hidden_width), BF16),
            ((tok_rows, hidden_width), BF16),
            half_low,
            half_low,
        ],
        [x_local, attn_mine, attn_other, ffn_gain_row, w_gate, w_up, grad_hidden],
        "v" * 7,
    )
    chip = chip_sum(part_mine, part_other)
    n2_mine, n2_other = slice_sum(chip)

    shard = width // devices
    y_width = hidden_width * 7 // 9 // LANES * LANES
    gate_cut = hidden_width // 3 // LANES * LANES
    gate_at = 2 * hidden_width - y_width
    z_width = gate_at + gate_cut
    ffn_mine, ffn_other, y_kept, y_sent, z_kept, z_sent = feed_grads(
        out_grad, normed_two, hidden, grad_gate, grad_upper, w_down, y_width, z_width, [chip]
    )
    ffn_chip = hold(chip_sum(ffn_mine, ffn_other), [n2_mine])
    y_received = flip(y_sent, "ctx", 1)
    z_received = flip(z_sent, "ctx", 2)

    grad_other, grad_query_t, grad_middle, grad_middle_low, grad_attended, ffn_gain_part = (
        call_kernel(
            functools.partial(back_first_kernel, devices, head_dim, wt_count),
            [
                ((pairs, tok_rows, 2 * kv_width), BF16),
                ((2, LANES, stacked), F32),
                ((tok_rows, width), F32),
                ((tok_rows, width), BF16),
                ((tok_rows, q_width), BF16),
                ((1, width), F32),
            ],
            place
            + [query, out_wide, log_total, middle, n2_mine, n2_other, out_grad, ffn_gain_row, w_out]
            + other_slots,
            "ss" + "v" * 9 + "a" * pairs,
            [
                held,
                spread,
                spread,
                pltpu.VMEM((2, 8, stacked), F32),
                pltpu.VMEM((half_rows, 2 * LANES), F32),
                pltpu.SemaphoreType.DMA((pairs,)),
            ],
            after=[ffn_chip],
            )
    )
    ffn_mine, ffn_other = slice_sum(ffn_chip)
    grad_same, query_raw_low, query_gain_sum = call_kernel(
        functools.partial(back_second_kernel, devices, head_dim),
        [
            ((pairs, tok_rows, 2 * kv_width), BF16),
            ((tok_rows, q_width), BF16),
            ((1, LANES), F32),
        ],
        place
        + [query, grad_attended, out_wide, log_total, raw, query_gain_row]
        + tables
        + [grad_query_t]
        + same_slots,
        "ss" + "v" * 10 + "a" * (1 + pairs),
        [
            held,
            spread,
            spread,
            pltpu.VMEM((2, 8, stacked), F32),
            pltpu.VMEM((2, LANES, stacked), F32),
            pltpu.VMEM((half_rows, 2 * LANES), F32),
            pltpu.SemaphoreType.DMA((pairs + 1,)),
        ],
        after=[ffn_mine],
    )
    bits = list(ctx_bits())
    key_value_received = flip(grad_other, "ctx", 1)
    y_kept, y_sent = halve(hold(y_kept, [grad_same]), y_received, bits[1:], 1)
    y_received = flip(y_sent, "ctx", 2)
    first_kept, first_sent = call_kernel(
        functools.partial(narrow_grad_kernel, devices, (gate_cut, 0, 0)),
        [((pairs, shard, hidden_width - gate_cut + 2 * q_width), BF16)] * 2,
        [normed_two, grad_gate, normed_one, query_raw_low, grad_middle_low, out_low],
        "v" * 6,
        after=[y_sent],
    )
    z_kept, z_sent = halve(hold(z_kept, [first_sent]), z_received, bits[:1] + bits[2:], 0)
    z_received = flip(z_sent, "ctx", 1)
    key_value_kept = hold(grad_same, [z_sent])
    key_value_sends = []
    rest = bits[1:]
    for bit in bits[1:]:
        key_value_kept, sent = halve(key_value_kept, key_value_received, rest, bit)
        rest.remove(bit)
        key_value_received = flip(sent, "ctx", 1 << bit)
        key_value_sends.append(sent)
    first_received = flip(hold(first_sent, key_value_sends[:1]), "ctx", 1)
    z_kept, z_sent = halve(hold(z_kept, key_value_sends[1:2]), z_received, bits[2:], bits[2])
    z_received = flip(z_sent, "ctx", 1 << bits[2])
    y_total, _ = scatter_tail(hold(y_kept, key_value_sends[:1]), y_received, bits[2:])

    grad_key_value_low, part_mine, part_other, gains = call_kernel(
        functools.partial(key_back_kernel, devices, head_dim, 2),
        [
            ((tok_rows, 2 * kv_width), BF16),
            half_low,
            half_low,
            ((1, 2 * width + 2 * LANES), F32),
        ],
        place
        + [raw, key_gain_row]
        + tables
        + [query_raw_low, x_local, w_query, w_key, w_value, ffn_gain_part, query_gain_sum]
        + [key_value_kept[0], key_value_received[0]],
        "ss" + "v" * 15,
        after=[y_total, z_sent],
    )
    n1_chip = chip_sum(part_mine, part_other)
    n1_received = flip(n1_chip, "wt", 2)

    second_kept, second_sent = call_kernel(
        functools.partial(narrow_grad_kernel, devices, (0,)),
        [((pairs, shard + GAIN_ROWS, 2 * kv_width), BF16)] * 2,
        [normed_one, grad_key_value_low, gains],
        "v" * 3,
        after=[n1_chip],
    )
    first_kept, first_sent = halve(hold(first_kept, [second_sent]), first_received, bits[1:], 1)
    first_received = flip(first_sent, "ctx", 2)
    n1_mine = (hold(n1_chip, [first_sent]).astype(F32) + n1_received.astype(F32)).astype(BF16)
    n1_other = flip(n1_mine, "wt", 1)
    second_kept, second_sent = halve(
        hold(second_kept, [n1_mine]), flip(second_sent, "ctx", 1), bits[1:], 1
    )
    second_received = flip(second_sent, "ctx", 2)
    (grad_input,) = call_kernel(
        finish_kernel,
        [((tok_rows, width), F32)],
        [x_local, n1_mine, n1_other, attn_gain_row, grad_middle],
        "v" * 5,
        after=[second_sent],
    )
    first, first_sends = scatter_tail(hold(first_kept, [grad_input]), first_received, bits[2:])
    second, second_sends = scatter_tail(
        hold(second_kept, first_sends[-1:]), second_received, bits[2:]
    )
    z_total, _ = scatter_tail_from(hold(z_kept, second_sends[-1:]), z_received, bits[2:])
    gain_rows = second[shard : shard + 2]
    gain_rows = sum([flip(gain_rows, "wt", other_wt) for other_wt in range(1, wt_count)], gain_rows)

    def head_gain(at):
        row = jnp.sum(gain_rows[1, at * LANES : (at + 1) * LANES].reshape(-1, head_dim), axis=0)
        return lax.dynamic_slice_in_dim(row, ctx * (head_dim // devices), head_dim // devices)

    gate_rest = hidden_width - gate_cut
    ffn_mine = hold(ffn_mine, [n1_mine])
    out_mine = (middle[mine] + ffn_mine.astype(F32)).astype(BF16)
    out_other = (middle[other] + ffn_other.astype(F32)).astype(BF16)
    return (
        jnp.concatenate(
            [jnp.where(core == 0, out_mine, out_other), jnp.where(core == 0, out_other, out_mine)],
            axis=0,
        ),
        grad_input,
        first[:, gate_rest : gate_rest + q_width],
        second[:shard, :kv_width],
        second[:shard, kv_width:],
        first[:, gate_rest + q_width :].T,
        jnp.concatenate([z_total[:, gate_at:], first[:, :gate_rest]], axis=1),
        jnp.concatenate([y_total, z_total[:, hidden_width:gate_at]], axis=1),
        z_total[:, :hidden_width].T,
        gain_rows[0, :shard],
        gain_rows[0, LANES : LANES + shard],
        head_gain(0),
        head_gain(1),
    )


def solution(mesh):
    in_specs = (
        P("ctx", None),
        P(),
        P(),
        P(None, "wt"),
        P(None, "wt"),
        P(None, "wt"),
        P("wt", None),
        P(None, "wt"),
        P(None, "wt"),
        P("wt", None),
        P(),
        P(),
        P(),
        P(),
        P("ctx", None),
    )
    out_specs = (
        P("ctx", None),
        P("ctx", None),
        P("ctx", "wt"),
        P("ctx", "wt"),
        P("ctx", "wt"),
        P("wt", "ctx"),
        P("ctx", "wt"),
        P("ctx", "wt"),
        P("wt", "ctx"),
        P("ctx"),
        P("ctx"),
        P("ctx"),
        P("ctx"),
    )
    return jax.shard_map(
        on_device, mesh=mesh, in_specs=in_specs, out_specs=out_specs, check_vma=False
    )
```

profile of v0, /device:TPU:0, one launch (start us, length us, event | category | flops | bytes accessed | tf_op | source)
XLA Modules:
  0.0 264.7 jit_solution(13455490372899882648)
XLA Ops:
  0.7 4.9 %shard_map.282 = (bf16[512,256]{1,0:T(8,128)(2,1)}, bf16[512,256]{1,0:T(8,128)(2,1)}, f32[512,384]{1,0:T(8,128)}, bf16[512,1024]{1,0:T(8,128)(2,1)}, bf16[512,1024]{1,0:T(8,128)(2,1)}, /*index=5*/s32[4]{0:T(128)}) custom-call(s32[16]{0:T(128)} %refs_0_.11, bf16[512,1024]{1,0:T(8,128)(2,1)} %refs_1_.1, s32[32,128]{1,0:T(8,128)} %bitcast.114, ...), custom_call_target="tpu_custom_call" | custom-call | flops 1000 | tf_op jit(solution)/shard_map/pallas_call | solution.py:633
  5.5 3.1 %collective-permute-start = (bf16[512,256]{1,0:T(8,128)(2,1)}, bf16[512,256]{1,0:T(8,128)(2,1)S(1)}, u32[]{:S(2)}, u32[]{:S(2)}) collective-permute-start(bf16[512,256]{1,0:T(8,128)(2,1)} %get-tuple-element.59.refs_3_.refs_13_), channel_id=1, source_target_pairs={{0,8},{4,12},{8,16},{12,20},{16,24},{20,28},{24,0},{28,4},{1,9},{5... | collective-permute-start | bytes 786440 | tf_op jit(solution)/shard_map/ppermute | solution.py:662
  14.6 3.5 %collective-permute-done.refs_4_.refs_14_ = bf16[512,256]{1,0:T(8,128)(2,1)S(1)} collective-permute-done((bf16[512,256]{1,0:T(8,128)(2,1)}, bf16[512,256]{1,0:T(8,128)(2,1)S(1)}, u32[]{:S(2)}, u32[]{:S(2)}) %collective-permute-start) | collective-permute-done | bytes 262176 | tf_op jit(solution)/shard_map/ppermute | solution.py:662
  19.9 8.6 %collective-permute-done.1.refs_5_.refs_15_ = bf16[512,256]{1,0:T(8,128)(2,1)S(1)} collective-permute-done((bf16[512,256]{1,0:T(8,128)(2,1)}, bf16[512,256]{1,0:T(8,128)(2,1)S(1)}, u32[]{:S(2)}, u32[]{:S(2)}) %collective-permute-start.1) | collective-permute-done | bytes 262176 | tf_op jit(solution)/shard_map/ppermute | solution.py:662
  30.6 3.0 %fusion.15.refs_8_.refs_6_ = f32[512,1152]{1,0:T(8,128)} fusion(bf16[512,1024]{1,0:T(8,128)(2,1)S(1)} %maximum_select_fusion.c_ref.refs_8_, bf16[1152,1024]{1,0:T(8,128)(2,1)S(1)} %copy-done.33), kind=kOutput, calls=%fused_computation.63 | convolution fusion | flops 1207959552 | bytes 5767168 | tf_op jit(solution)/shard_map/dot_general | solution.py:30
  34.3 10.5 %shard_map.283 = (f32[2,1024,256]{2,1,0:T(8,128)}, bf16[2,1024,128]{2,1,0:T(8,128)(2,1)}) custom-call(s32[16]{0:T(128)} %refs_0_.11, s32[4]{0:T(128)} %get-tuple-element.57.refs_1_, bf16[512,256]{1,0:T(8,128)(2,1)} %get-tuple-element.58.refs_2_, bf16[512,256]{1,0:T(8,128)(2,1)} %get-tuple-element.59.refs_3_.refs_13_, bf16[512,256]{1,0:T(8,128)(2,1)} %copy-done.19, ...), custom_call_target="tpu_custom_call" | custom-call | flops 1000 | tf_op jit(solution)/shard_map/pallas_call | solution.py:633
  45.7 8.2 %shard_map.284 = (bf16[512,256]{1,0:T(8,128)(2,1)}, f32[512,256]{1,0:T(8,128)}, f32[2,8,1024]{2,1,0:T(8,128)}, bf16[256,1024]{1,0:T(8,128)(2,1)}, bf16[256,1024]{1,0:T(8,128)(2,1)}) custom-call(s32[16]{0:T(128)} %refs_0_.11, s32[4]{0:T(128)} %get-tuple-element.57.refs_1_, bf16[2,1024,128]{2,1,0:T(8,128)(2,1)} %get-tuple-element.60.refs_2_, ...), custom_call_target="tpu_custom_call" | custom-call | flops 1000 | tf_op jit(solution)/shard_map/pallas_call | solution.py:633
  58.9 12.5 %collective-permute-done.8 = bf16[256,1024]{1,0:T(8,128)(2,1)S(1)} collective-permute-done((bf16[256,1024]{1,0:T(8,128)(2,1)S(1)}, bf16[256,1024]{1,0:T(8,128)(2,1)S(1)}, u32[]{:S(2)}, u32[]{:S(2)}) %collective-permute-start.8) | collective-permute-done | bytes 524320 | tf_op jit(solution)/shard_map/ppermute | solution.py:657
  74.3 10.9 %shard_map.285 = (f32[512,1024]{1,0:T(8,128)}, bf16[512,1024]{1,0:T(8,128)(2,1)}, bf16[512,1152]{1,0:T(8,128)(2,1)}, bf16[512,1152]{1,0:T(8,128)(2,1)}, bf16[512...) custom-call(bf16[512,1024]{1,0:T(8,128)(2,1)} %get-tuple-element.56.refs_0_.refs_9_, ...), custom_call_target="tpu_custom_call" | custom-call | flops 1000 | tf_op jit(solution)/shard_map/pallas_call | solution.py:633
  90.2 11.9 %shard_map.286 = (bf16[256,1024]{1,0:T(8,128)(2,1)}, bf16[256,1024]{1,0:T(8,128)(2,1)}, bf16[4,128,896]{2,1,0:T(8,128)(2,1)}, bf16[4,128,896]{2,1,0:T(8,128)(2,1...) custom-call(bf16[512,1024]{1,0:T(8,128)(2,1)} %copy-done.8, ...), custom_call_target="tpu_custom_call" | custom-call | flops 14000000000 | tf_op jit(solution)/shard_map/pallas_call | solution.py:574
  102.1 5.6 %collective-permute-start.16 = (bf16[4,128,1792]{2,1,0:T(8,128)(2,1)}, bf16[4,128,1792]{2,1,0:T(8,128)(2,1)S(1)}, u32[]{:S(2)}, u32[]{:S(2)}) collective-permute-start(bf16[4,128,1792]{2,1,0:T(8,128)(2,1)} %get-tuple-element.89), channel_id=1, source_target_pairs={{0,8},{4,12},{8,0},{12,4},{16,24},{20,28},{24,16},{28,20},{1,9},{5... | collective-permute-start | bytes 5505032 | tf_op jit(solution)/shard_map/ppermute | solution.py:657
  111.9 14.7 %shard_map.288 = (bf16[4,512,256]{2,1,0:T(8,128)(2,1)}, f32[2,128,1024]{2,1,0:T(8,128)}, f32[512,1024]{1,0:T(8,128)}, bf16[512,1024]{1,0:T(8,128)(2,1)}, bf16[512,256]{1,0:T(8,128)(2,1)}, /*index=5*/f32[1,1024]{1,0:T(1,128)}) custom-call(s32[16]{0:T(128)} %refs_0_.11, s32[4]{0:T(128)} %get-tuple-element.57.refs_1_, ...), custom_call_target="tpu_custom_call" | custom-call | flops 1000 | tf_op jit(solution)/shard_map/pallas_call | solution.py:633
  127.8 12.7 %shard_map.289 = (bf16[4,512,256]{2,1,0:T(8,128)(2,1)}, bf16[512,256]{1,0:T(8,128)(2,1)}, f32[1,128]{1,0:T(1,128)}) custom-call(s32[16]{0:T(128)} %refs_0_.11, s32[4]{0:T(128)} %get-tuple-element.57.refs_1_, bf16[512,256]{1,0:T(8,128)(2,1)} %get-tuple-element.58.refs_2_, bf16[512,256]{1,0:T(8,128)(2,1)} %get-tuple-element.76.refs_3_, ...), custom_call_target="tpu_custom_call" | custom-call | flops 1000 | tf_op jit(solution)/shard_map/pallas_call | solution.py:633
  145.6 8.6 %shard_map.291 = (bf16[4,128,1280]{2,1,0:T(8,128)(2,1)}, bf16[4,128,1280]{2,1,0:T(8,128)(2,1)}) custom-call(bf16[512,1024]{1,0:T(8,128)(2,1)} %get-tuple-element.65.n2_ref.refs_0_, bf16[512,1152]{1,0:T(8,128)(2,1)} %get-tuple-element.67.dgate_ref.refs_1_, bf16[512,1024]{1,0:T(8,128)(2,1)} %get-tuple-element.83.refs_2_.refs_0_, ...), custom_call_target="tpu_custom_call" | custom-call | flops 1000 | tf_op jit(solution)/shard_map/pallas_call | solution.py:633
  154.2 3.2 %fusion.1 = (bf16[2,128,1792]{2,1,0:T(8,128)(2,1)}, bf16[2,128,1792]{2,1,0:T(8,128)(2,1)}) fusion(bf16[2,2,1,128,1792]{4,3,1,0,2:T(8,128)(2,1)S(1)} %bitcast.107, s32[]{:T(128)S(6)} %select_n.148, bf16[2,2,1,128,1792]{4,3,1,0,2:T(8,128)(2,1)} %bitcast.104, s32[]{:T(128)S(6)} %select_n.142), kind=kLoop, calls=%fused_computation.19 | loop fusion | flops 3670016 | bytes 5505032 | tf_op jit(solution)/shard_map/convert_element_type | solution.py:690
  165.0 13.9 %collective-permute-done.18 = bf16[2,512,256]{2,1,0:T(8,128)(2,1)} collective-permute-done((bf16[2,512,256]{2,1,0:T(8,128)(2,1)S(1)}, bf16[2,512,256]{2,1,0:T(8,128)(2,1)}, u32[]{:S(2)}, u32[]{:S(2)}) %collective-permute-start.18) | collective-permute-done | bytes 524320 | tf_op jit(solution)/shard_map/ppermute | solution.py:657
  185.2 7.4 %collective-permute-done.19 = bf16[1,512,256]{2,1,0:T(8,128)(2,1)S(1)} collective-permute-done((bf16[1,512,256]{2,1,0:T(8,128)(2,1)S(1)}, bf16[1,512,256]{2,1,0:T(8,128)(2,1)S(1)}, u32[]{:S(2)}, u32[]{:S(2)}) %collective-permute-start.19) | collective-permute-done | bytes 262176 | tf_op jit(solution)/shard_map/ppermute | solution.py:657
  193.3 4.6 %shard_map.296 = (bf16[512,256]{1,0:T(8,128)(2,1)}, bf16[256,1024]{1,0:T(8,128)(2,1)}, bf16[256,1024]{1,0:T(8,128)(2,1)}, f32[1,2304]{1,0:T(1,128)}) custom-call(s32[16]{0:T(128)} %refs_0_.11, s32[4]{0:T(128)} %get-tuple-element.57.refs_1_, f32[512,384]{1,0:T(8,128)} %get-tuple-element.73.refs_6_.refs_2_, f32[1,64]{1,0:T(1,128)} %bitcast.120, ...), custom_call_target="tpu_custom_call" | custom-call | flops 1000 | tf_op jit(solution)/shard_map/pallas_call | solution.py:633
  202.3 3.4 %shard_map.297 = (bf16[4,144,256]{2,1,0:T(8,128)(2,1)}, bf16[4,144,256]{2,1,0:T(8,128)(2,1)}) custom-call(bf16[512,1024]{1,0:T(8,128)(2,1)} %get-tuple-element.83.refs_2_.refs_0_, bf16[512,256]{1,0:T(8,128)(2,1)} %get-tuple-element.94.refs_1_, f32[1,2304]{1,0:T(1,128)} %get-tuple-element.95.refs_2_, bf16[256,1024]{1,0:T(8,128)(2,1)} %copy-done), custom_call_target="tpu_custom_call" | custom-call | flops 1000 | tf_op jit(solution)/shard_map/pallas_call | solution.py:633
  208.3 3.0 %fusion.3 = (bf16[2,128,1280]{2,1,0:T(8,128)(2,1)}, bf16[2,128,1280]{2,1,0:T(8,128)(2,1)}) fusion(bf16[2,2,1,128,1280]{4,3,1,0,2:T(8,128)(2,1)} %bitcast.25, s32[]{:T(128)S(6)} %select_n.143, bf16[2,2,1,128,1280]{4,3,1,0,2:T(8,128)(2,1)} %bitcast.105, s32[]{:T(128)S(6)} %select_n.140), kind=kLoop, calls=%fused_computation.26 | loop fusion | flops 2621440 | bytes 3932168 | tf_op jit(solution)/shard_map/convert_element_type | solution.py:690
  212.4 2.9 %collective-permute-done.25 = bf16[256,1024]{1,0:T(8,128)(2,1)S(1)} collective-permute-done((bf16[256,1024]{1,0:T(8,128)(2,1)S(1)}, bf16[256,1024]{1,0:T(8,128)(2,1)S(1)}, u32[]{:S(2)}, u32[]{:S(2)}) %collective-permute-start.25) | collective-permute-done | bytes 524320 | tf_op jit(solution)/shard_map/ppermute | solution.py:657
  222.7 4.5 %shard_map.303.refs_1_ = f32[512,1024]{1,0:T(8,128)} custom-call(bf16[512,1024]{1,0:T(8,128)(2,1)} %get-tuple-element.56.refs_0_.refs_9_, bf16[256,1024]{1,0:T(8,128)(2,1)} %copy-done.4, bf16[256,1024]{1,0:T(8,128)(2,1)} %collective-permute-done.27.refs_2_, f32[1,1024]{1,0:T(1,128)} %bitcast.116, f32[512,1024]{1,0:T(8,128)} %get-tuple-element.97.refs_4_, ...), custom_call_target="tpu_custom_call" | custom-call | flops 1000 | tf_op jit(solution)/shard_map/pallas_call | solution.py:633
  227.2 11.8 %collective-permute-done.29 = bf16[2,128,1280]{2,1,0:T(8,128)(2,1)} collective-permute-done((bf16[2,128,1280]{2,1,0:T(8,128)(2,1)}, bf16[2,128,1280]{2,1,0:T(8,128)(2,1)}, u32[]{:S(2)}, u32[]{:S(2)}) %collective-permute-start.29) | collective-permute-done | bytes 655392 | tf_op jit(solution)/shard_map/ppermute | solution.py:657
  248.1 6.7 %collective-permute-done.32 = bf16[1,144,256]{2,1,0:T(8,128)(2,1)S(1)} collective-permute-done((bf16[1,144,256]{2,1,0:T(8,128)(2,1)S(1)}, bf16[1,144,256]{2,1,0:T(8,128)(2,1)S(1)}, u32[]{:S(2)}, u32[]{:S(2)}) %collective-permute-start.32) | collective-permute-done | bytes 73760 | tf_op jit(solution)/shard_map/ppermute | solution.py:657
  (190 shorter events, 82.9 us)
Async XLA Ops:
  8.6 19.9 %collective-permute-start.1 = (bf16[512,256]{1,0:T(8,128)(2,1)}, bf16[512,256]{1,0:T(8,128)(2,1)S(1)}, u32[]{:S(2)}, u32[]{:S(2)}) collective-permute-start(bf16[512,256]{1,0:T(8,128)(2,1)} %get-tuple-element.59.refs_3_.refs_13_), channel_id=1, source_target_pairs={{0,16},{4,20},{8,24},{12,28},{16,0},{20,4},{24,8},{28,12},{1,17},{... | collective-permute-start | bytes 786440 | tf_op jit(solution)/shard_map/ppermute | solution.py:662
  11.2 18.8 %collective-permute-start.2 = (bf16[512,256]{1,0:T(8,128)(2,1)}, bf16[512,256]{1,0:T(8,128)(2,1)S(1)}, u32[]{:S(2)}, u32[]{:S(2)}) collective-permute-start(bf16[512,256]{1,0:T(8,128)(2,1)} %get-tuple-element.59.refs_3_.refs_13_), channel_id=1, source_target_pairs={{0,24},{4,28},{8,0},{12,4},{16,8},{20,12},{24,16},{28,20},{1,25},{... | collective-permute-start | bytes 786440 | tf_op jit(solution)/shard_map/ppermute | solution.py:662
  12.6 21.0 %collective-permute-start.3 = (bf16[512,256]{1,0:T(8,128)(2,1)}, bf16[512,256]{1,0:T(8,128)(2,1)S(1)}, u32[]{:S(2)}, u32[]{:S(2)}) collective-permute-start(bf16[512,256]{1,0:T(8,128)(2,1)} %get-tuple-element.59.refs_3_.refs_13_), channel_id=1, source_target_pairs={{0,4},{4,0},{8,12},{12,8},{16,20},{20,16},{24,28},{28,24},{1,5},{5... | collective-permute-start | bytes 786440 | tf_op jit(solution)/shard_map/ppermute | solution.py:657
  18.1 26.6 %collective-permute-start.4 = (bf16[512,256]{1,0:T(8,128)(2,1)S(1)}, bf16[512,256]{1,0:T(8,128)(2,1)S(1)}, u32[]{:S(2)}, u32[]{:S(2)}) collective-permute-start(bf16[512,256]{1,0:T(8,128)(2,1)S(1)} %collective-permute-done.refs_4_.refs_14_), channel_id=1, source_target_pairs={{0,4},{4,0},{8,12},{12,8},{16,20},{20,16},{24,28},{28,24},{1,5},{5... | collective-permute-start | bytes 786440 | tf_op jit(solution)/shard_map/ppermute | solution.py:657
  28.5 16.2 %collective-permute-start.5 = (bf16[512,256]{1,0:T(8,128)(2,1)S(1)}, bf16[512,256]{1,0:T(8,128)(2,1)S(1)}, u32[]{:S(2)}, u32[]{:S(2)}) collective-permute-start(bf16[512,256]{1,0:T(8,128)(2,1)S(1)} %collective-permute-done.1.refs_5_.refs_15_), channel_id=1, source_target_pairs={{0,4},{4,0},{8,12},{12,8},{16,20},{20,16},{24,28},{28,24},{1,5},{5... | collective-permute-start | bytes 786440 | tf_op jit(solution)/shard_map/ppermute | solution.py:657
  30.1 14.7 %collective-permute-start.6 = (bf16[512,256]{1,0:T(8,128)(2,1)S(1)}, bf16[512,256]{1,0:T(8,128)(2,1)S(1)}, u32[]{:S(2)}, u32[]{:S(2)}) collective-permute-start(bf16[512,256]{1,0:T(8,128)(2,1)S(1)} %collective-permute-done.2.refs_6_.refs_16_), channel_id=1, source_target_pairs={{0,4},{4,0},{8,12},{12,8},{16,20},{20,16},{24,28},{28,24},{1,5},{5... | collective-permute-start | bytes 786440 | tf_op jit(solution)/shard_map/ppermute | solution.py:657
  57.3 14.0 %collective-permute-start.8 = (bf16[256,1024]{1,0:T(8,128)(2,1)S(1)}, bf16[256,1024]{1,0:T(8,128)(2,1)S(1)}, u32[]{:S(2)}, u32[]{:S(2)}) collective-permute-start(bf16[256,1024]{1,0:T(8,128)(2,1)S(1)} %add_convert_fusion.15), channel_id=1, source_target_pairs={{0,2},{1,3},{2,0},{3,1},{4,6},{5,7},{6,4},{7,5},{8,10},{9,11},{10,... | collective-permute-start | bytes 1572872 | tf_op jit(solution)/shard_map/ppermute | solution.py:657
  88.6 19.2 %collective-permute-start.12 = (bf16[256,1024]{1,0:T(8,128)(2,1)S(1)}, bf16[256,1024]{1,0:T(8,128)(2,1)S(1)}, u32[]{:S(2)}, u32[]{:S(2)}) collective-permute-start(bf16[256,1024]{1,0:T(8,128)(2,1)S(1)} %add_convert_fusion.13.refs_0_), channel_id=1, source_target_pairs={{0,2},{1,3},{2,0},{3,1},{4,6},{5,7},{6,4},{7,5},{8,10},{9,11},{10,... | collective-permute-start | bytes 1572872 | tf_op jit(solution)/shard_map/ppermute | solution.py:657
  102.1 52.1 %collective-permute-start.16 = (bf16[4,128,1792]{2,1,0:T(8,128)(2,1)}, bf16[4,128,1792]{2,1,0:T(8,128)(2,1)S(1)}, u32[]{:S(2)}, u32[]{:S(2)}) collective-permute-start(bf16[4,128,1792]{2,1,0:T(8,128)(2,1)} %get-tuple-element.89), channel_id=1, source_target_pairs={{0,8},{4,12},{8,0},{12,4},{16,24},{20,28},{24,16},{28,20},{1,9},{5... | collective-permute-start | bytes 5505032 | tf_op jit(solution)/shard_map/ppermute | solution.py:657
  109.6 31.0 %collective-permute-start.15 = (bf16[4,128,896]{2,1,0:T(8,128)(2,1)}, bf16[4,128,896]{2,1,0:T(8,128)(2,1)}, u32[]{:S(2)}, u32[]{:S(2)}) collective-permute-start(bf16[4,128,896]{2,1,0:T(8,128)(2,1)} %get-tuple-element.87), channel_id=1, source_target_pairs={{0,4},{4,0},{8,12},{12,8},{16,20},{20,16},{24,28},{28,24},{1,5},{5... | collective-permute-start | bytes 2752520 | tf_op jit(solution)/shard_map/ppermute | solution.py:657
  111.2 15.6 %collective-permute-start.13 = (bf16[256,1024]{1,0:T(8,128)(2,1)}, bf16[256,1024]{1,0:T(8,128)(2,1)S(1)}, u32[]{:S(2)}, u32[]{:S(2)}) collective-permute-start(bf16[256,1024]{1,0:T(8,128)(2,1)} %shard_map.287.refs_15_), channel_id=1, source_target_pairs={{0,2},{1,3},{2,0},{3,1},{4,6},{5,7},{6,4},{7,5},{8,10},{9,11},{10,... | collective-permute-start | bytes 1572872 | tf_op jit(solution)/shard_map/ppermute | solution.py:657
  126.7 32.4 %collective-permute-start.17 = (bf16[4,512,256]{2,1,0:T(8,128)(2,1)}, bf16[4,512,256]{2,1,0:T(8,128)(2,1)}, u32[]{:S(2)}, u32[]{:S(2)}) collective-permute-start(bf16[4,512,256]{2,1,0:T(8,128)(2,1)} %get-tuple-element.90), channel_id=1, source_target_pairs={{0,4},{4,0},{8,12},{12,8},{16,20},{20,16},{24,28},{28,24},{1,5},{5... | collective-permute-start | bytes 3145736 | tf_op jit(solution)/shard_map/ppermute | solution.py:657
  143.0 18.6 %collective-permute-start.20 = (bf16[2,128,896]{2,1,0:T(8,128)(2,1)S(1)}, bf16[2,128,896]{2,1,0:T(8,128)(2,1)}, u32[]{:S(2)}, u32[]{:S(2)}) collective-permute-start(bf16[2,128,896]{2,1,0:T(8,128)(2,1)S(1)} %get-tuple-element.138.refs_6_), channel_id=1, source_target_pairs={{0,8},{4,12},{8,0},{12,4},{16,24},{20,28},{24,16},{28,20},{1,9},{5... | collective-permute-start | bytes 1376264 | tf_op jit(solution)/shard_map/ppermute | solution.py:657
  158.5 24.3 %collective-permute-start.22 = (bf16[2,128,1792]{2,1,0:T(8,128)(2,1)S(1)}, bf16[2,128,1792]{2,1,0:T(8,128)(2,1)S(1)}, u32[]{:S(2)}, u32[]{:S(2)}) collective-permute-start(bf16[2,128,1792]{2,1,0:T(8,128)(2,1)S(1)} %copy-done.13), channel_id=1, source_target_pairs={{0,4},{4,0},{8,12},{12,8},{16,20},{20,16},{24,28},{28,24},{1,5},{5... | collective-permute-start | bytes 2752520 | tf_op jit(solution)/shard_map/ppermute | solution.py:657
  160.8 18.1 %collective-permute-start.18 = (bf16[2,512,256]{2,1,0:T(8,128)(2,1)S(1)}, bf16[2,512,256]{2,1,0:T(8,128)(2,1)}, u32[]{:S(2)}, u32[]{:S(2)}) collective-permute-start(bf16[2,512,256]{2,1,0:T(8,128)(2,1)S(1)} %get-tuple-element.134.refs_1_), channel_id=1, source_target_pairs={{0,8},{4,12},{8,0},{12,4},{16,24},{20,28},{24,16},{28,20},{1,9},{5... | collective-permute-start | bytes 1572872 | tf_op jit(solution)/shard_map/ppermute | solution.py:657
  163.5 17.3 %collective-permute-start.21 = (bf16[1,128,896]{2,1,0:T(8,128)(2,1)}, bf16[1,128,896]{2,1,0:T(8,128)(2,1)}, u32[]{:S(2)}, u32[]{:S(2)}) collective-permute-start(bf16[1,128,896]{2,1,0:T(8,128)(2,1)} %add_convert_fusion.22), channel_id=1, source_target_pairs={{0,16},{4,20},{8,24},{12,28},{16,0},{20,4},{24,8},{28,12},{1,17},{... | collective-permute-start | bytes 688136 | tf_op jit(solution)/shard_map/ppermute | solution.py:657
  163.5 44.8 %collective-permute-start.24 = (bf16[4,128,1280]{2,1,0:T(8,128)(2,1)}, bf16[4,128,1280]{2,1,0:T(8,128)(2,1)}, u32[]{:S(2)}, u32[]{:S(2)}) collective-permute-start(bf16[4,128,1280]{2,1,0:T(8,128)(2,1)} %shard_map.299), channel_id=1, source_target_pairs={{0,4},{4,0},{8,12},{12,8},{16,20},{20,16},{24,28},{28,24},{1,5},{5... | collective-permute-start | bytes 3932168 | tf_op jit(solution)/shard_map/ppermute | solution.py:657
  201.3 14.0 %collective-permute-start.25 = (bf16[256,1024]{1,0:T(8,128)(2,1)S(1)}, bf16[256,1024]{1,0:T(8,128)(2,1)S(1)}, u32[]{:S(2)}, u32[]{:S(2)}) collective-permute-start(bf16[256,1024]{1,0:T(8,128)(2,1)S(1)} %add_convert_fusion.7.refs_3_.refs_0_), channel_id=1, source_target_pairs={{0,2},{1,3},{2,0},{3,1},{4,6},{5,7},{6,4},{7,5},{8,10},{9,11},{10,... | collective-permute-start | bytes 1572872 | tf_op jit(solution)/shard_map/ppermute | solution.py:657
  202.3 17.8 %collective-permute-start.26 = (bf16[256,1024]{1,0:T(8,128)(2,1)S(1)}, bf16[256,1024]{1,0:T(8,128)(2,1)}, u32[]{:S(2)}, u32[]{:S(2)}) collective-permute-start(bf16[256,1024]{1,0:T(8,128)(2,1)S(1)} %copy-done.3), channel_id=1, source_target_pairs={{0,1},{1,0},{2,3},{3,2},{4,5},{5,4},{6,7},{7,6},{8,9},{9,8},{10,11... | collective-permute-start | bytes 1572872 | tf_op jit(solution)/shard_map/ppermute | solution.py:657
  202.3 40.1 %collective-permute-start.33 = (bf16[1,128,1792]{2,1,0:T(8,128)(2,1)}, bf16[1,128,1792]{2,1,0:T(8,128)(2,1)}, u32[]{:S(2)}, u32[]{:S(2)}) collective-permute-start(bf16[1,128,1792]{2,1,0:T(8,128)(2,1)} %get-tuple-element.136.refs_18_), channel_id=1, source_target_pairs={{0,16},{4,20},{8,24},{12,28},{16,0},{20,4},{24,8},{28,12},{1,17},{... | collective-permute-start | bytes 1376264 | tf_op jit(solution)/shard_map/ppermute | solution.py:657
  211.3 27.6 %collective-permute-start.29 = (bf16[2,128,1280]{2,1,0:T(8,128)(2,1)}, bf16[2,128,1280]{2,1,0:T(8,128)(2,1)}, u32[]{:S(2)}, u32[]{:S(2)}) collective-permute-start(bf16[2,128,1280]{2,1,0:T(8,128)(2,1)} %get-tuple-element.132.refs_1_), channel_id=1, source_target_pairs={{0,8},{4,12},{8,0},{12,4},{16,24},{20,28},{24,16},{28,20},{1,9},{5... | collective-permute-start | bytes 1966088 | tf_op jit(solution)/shard_map/ppermute | solution.py:657
  220.0 20.8 %collective-permute-start.31 = (bf16[2,144,256]{2,1,0:T(8,128)(2,1)S(1)}, bf16[2,144,256]{2,1,0:T(8,128)(2,1)S(1)}, u32[]{:S(2)}, u32[]{:S(2)}) collective-permute-start(bf16[2,144,256]{2,1,0:T(8,128)(2,1)S(1)} %get-tuple-element.146.refs_5_), channel_id=1, source_target_pairs={{0,8},{4,12},{8,0},{12,4},{16,24},{20,28},{24,16},{28,20},{1,9},{5... | collective-permute-start | bytes 442376 | tf_op jit(solution)/shard_map/ppermute | solution.py:657
  241.7 13.1 %collective-permute-start.32 = (bf16[1,144,256]{2,1,0:T(8,128)(2,1)S(1)}, bf16[1,144,256]{2,1,0:T(8,128)(2,1)S(1)}, u32[]{:S(2)}, u32[]{:S(2)}) collective-permute-start(bf16[1,144,256]{2,1,0:T(8,128)(2,1)S(1)} %add_convert_fusion.26.refs_1_), channel_id=1, source_target_pairs={{0,16},{4,20},{8,24},{12,28},{16,0},{20,4},{24,8},{28,12},{1,17},{... | collective-permute-start | bytes 221192 | tf_op jit(solution)/shard_map/ppermute | solution.py:657
  243.8 17.1 %collective-permute-start.30 = (bf16[1,128,1280]{2,1,0:T(8,128)(2,1)S(1)}, bf16[1,128,1280]{2,1,0:T(8,128)(2,1)S(1)}, u32[]{:S(2)}, u32[]{:S(2)}) collective-permute-start(bf16[1,128,1280]{2,1,0:T(8,128)(2,1)S(1)} %copy-done.18), channel_id=1, source_target_pairs={{0,16},{4,20},{8,24},{12,28},{16,0},{20,4},{24,8},{28,12},{1,17},{... | collective-permute-start | bytes 983048 | tf_op jit(solution)/shard_map/ppermute | solution.py:657
  (48 other events, 259.7 us)
where the time goes:
time: 267 us; the launch traced here: 265 us
  Pallas kernels  94.9 us (36%)
  waiting for transfers between devices  78.1 us (29%)
  other arithmetic  38.6 us (14%)
  starting transfers between devices  36.9 us (14%)
  local copies, waits for them, and re-layouts  11.5 us (4%)
  matrix products  2.96 us (1%)
    pallas_call x10, Pallas kernels, call_kernel(): pl.pallas_call(whole, out_shape=[jax.ShapeDtypeStruct(shape, kind) for sh...  83 us
    ppermute x34, waiting for transfers between devices, flip(): return lax.ppermute(values, axis, [(i, i ^ bit) for i in range(size)])  66 us
    ppermute x34, starting transfers between devices, flip(): return lax.ppermute(values, axis, [(i, i ^ bit) for i in range(size)])  29.9 us
    convert_element_type x9, other arithmetic, pick(): return picked.astype(BF16).reshape((-1,) + view[3:])  19.2 us
    ppermute x3, waiting for transfers between devices, shift(): lax.ppermute(values, 'ctx', [(i, (i + step) % size) for i in range(size)])  12.1 us
    pallas_call x1, Pallas kernels, feed_grads(): pl.pallas_call(functools.partial(feed_grad_kernel, per_step), grid=(width...  11.9 us
    unnamed x70, local copies, waits for them, and re-layouts  8.18 us
    ppermute x3, starting transfers between devices, shift(): lax.ppermute(values, 'ctx', [(i, (i + step) % size) for i in range(size)])  7.01 us
  transfers between devices with their start and end apart: 37, of which 15 were waited for; matrix products, arithmetic and copies ran while one was open for 15% of the time, Pallas kernels for 27%

commit v1 on v0

--- a/solution.py
+++ b/solution.py
@@ -300,7 +300,8 @@
 
 
 def feed_kernel(x_ref, mine_ref, other_ref, gain_ref, wg_ref, wu_ref, dh_ref,
-                mid_ref, n2_ref, hid_ref, dgate_ref, dup_ref, part_mine, part_other):
+                mid_out, n2_out, hid_out, dgate_out, dup_out, part_mine, part_other,
+                mid_ref, n2_ref, hid_ref, dgate_ref, dup_ref, sems):
     rows = x_ref.shape[0] // 2
     hidden = wg_ref.shape[1]
     for half in range(2):
@@ -308,6 +309,7 @@
         middle = x_ref[here, :].astype(F32) + (mine_ref, other_ref)[half][...].astype(F32)
         mid_ref[here, :] = middle
         n2_ref[here, :] = rms_norm(middle, gain_ref[...]).astype(BF16)
+    early = fetch([(mid_ref, mid_out), (n2_ref, n2_out)], sems)
     step = 2 * LANES
     for at in range(0, hidden, step):
         cols = slice(at, min(at + step, hidden))
@@ -322,6 +324,7 @@
             grad_hidden * up * sigmoid * (1.0 + gate * (1.0 - sigmoid))
         ).astype(BF16)
         dup_ref[:, cols] = (grad_hidden * silu).astype(BF16)
+    late = fetch([(hid_ref, hid_out), (dgate_ref, dgate_out), (dup_ref, dup_out)], sems.at[2:5])
     for half, part in ((1, part_other), (0, part_mine)):
         here = half_slice(half, rows)
         for at in range(0, wg_ref.shape[0], step):
@@ -330,6 +333,8 @@
                 contract(dgate_ref[here, :], wg_ref[wide, :], 1, 1)
                 + contract(dup_ref[here, :], wu_ref[wide, :], 1, 1)
             ).astype(BF16)
+    for copy in early + late:
+        copy.wait()
 
 
 def prepare_back(info, head_dim, q_ref, do_ref, o32_ref, spread, spread_do, delta):
@@ -835,19 +840,14 @@
     )
     attn_mine, attn_other = slice_sum(chip_sum(attn_mine, attn_other))
 
+    feed_shapes = [((tok_rows, width), F32), ((tok_rows, width), BF16)]
+    feed_shapes += [((tok_rows, hidden_width), BF16)] * 3
     middle, normed_two, hidden, grad_gate, grad_upper, part_mine, part_other = call_kernel(
         feed_kernel,
-        [
-            ((tok_rows, width), F32),
-            ((tok_rows, width), BF16),
-            ((tok_rows, hidden_width), BF16),
-            ((tok_rows, hidden_width), BF16),
-            ((tok_rows, hidden_width), BF16),
-            half_low,
-            half_low,
-        ],
+        [(*shape, "a") for shape in feed_shapes] + [half_low, half_low],
         [x_local, attn_mine, attn_other, ffn_gain_row, w_gate, w_up, grad_hidden],
         "v" * 7,
+        [pltpu.VMEM(*shape) for shape in feed_shapes] + [pltpu.SemaphoreType.DMA((5,))],
     )
     chip = chip_sum(part_mine, part_other)
     n2_mine, n2_other = slice_sum(chip)

time: 267 us -> 268 us (level)
  Pallas kernels: 94.9 us -> 84.7 us
  starting transfers between devices: 36.9 us -> 45.2 us
    pallas_call x10, Pallas kernels: 83 us -> 72.8 us  [call_kernel(): pl.pallas_call(whole, out_shape=[jax.ShapeDtypeStruct(shape, kind) for sh...]
    ppermute x34, starting transfers between devices: 29.9 us -> 38.2 us  [flip(): return lax.ppermute(values, axis, [(i, i ^ bit) for i in range(size)])]
  transfers between devices with their start and end apart: 37 -> 37, of which waited for: 15 -> 19; matrix products, arithmetic and copies ran while one was open for 15% -> 15% of each run, Pallas kernels for 27% -> 24%
where the time goes in v1:
time: 268 us; the launch traced here: 264 us
  Pallas kernels  84.7 us (32%)
  waiting for transfers between devices  79.2 us (30%)
  starting transfers between devices  45.2 us (17%)
  other arithmetic  38.7 us (14%)
  local copies, waits for them, and re-layouts  11.4 us (4%)
  matrix products  2.96 us (1%)
    pallas_call x10, Pallas kernels, call_kernel(): pl.pallas_call(whole, out_shape=[jax.ShapeDtypeStruct(shape, kind) for sh...  72.8 us
    ppermute x34, waiting for transfers between devices, flip(): return lax.ppermute(values, axis, [(i, i ^ bit) for i in range(size)])  67 us
    ppermute x34, starting transfers between devices, flip(): return lax.ppermute(values, axis, [(i, i ^ bit) for i in range(size)])  38.2 us
    convert_element_type x9, other arithmetic, pick(): return picked.astype(BF16).reshape((-1,) + view[3:])  19.2 us
    ppermute x3, waiting for transfers between devices, shift(): lax.ppermute(values, 'ctx', [(i, (i + step) % size) for i in range(size)])  12.1 us
    pallas_call x1, Pallas kernels, feed_grads(): pl.pallas_call(functools.partial(feed_grad_kernel, per_step), grid=(width...  11.9 us
    unnamed x70, local copies, waits for them, and re-layouts  8.04 us
    ppermute x3, starting transfers between devices, shift(): lax.ppermute(values, 'ctx', [(i, (i + step) % size) for i in range(size)])  7.01 us
  transfers between devices with their start and end apart: 37, of which 19 were waited for; matrix products, arithmetic and copies ran while one was open for 15% of the time, Pallas kernels for 24%

profile of v1, /device:TPU:0, one launch (start us, length us, event | category | flops | bytes accessed | tf_op | source)
XLA Modules:
  0.0 263.7 jit_solution(2116329846198583065)
XLA Ops:
  0.7 4.9 %shard_map.282 = (bf16[512,256]{1,0:T(8,128)(2,1)}, bf16[512,256]{1,0:T(8,128)(2,1)}, f32[512,384]{1,0:T(8,128)}, bf16[512,1024]{1,0:T(8,128)(2,1)}, bf16[512,1024]{1,0:T(8,128)(2,1)}, /*index=5*/s32[4]{0:T(128)}) custom-call(s32[16]{0:T(128)} %refs_0_.11, bf16[512,1024]{1,0:T(8,128)(2,1)} %refs_1_.1, s32[32,128]{1,0:T(8,128)} %bitcast.114, ...), custom_call_target="tpu_custom_call" | custom-call | flops 1000 | tf_op jit(solution)/shard_map/pallas_call | solution.py:638
  5.5 3.1 %collective-permute-start = (bf16[512,256]{1,0:T(8,128)(2,1)}, bf16[512,256]{1,0:T(8,128)(2,1)S(1)}, u32[]{:S(2)}, u32[]{:S(2)}) collective-permute-start(bf16[512,256]{1,0:T(8,128)(2,1)} %get-tuple-element.59.refs_3_.refs_13_), channel_id=1, source_target_pairs={{0,8},{4,12},{8,16},{12,20},{16,24},{20,28},{24,0},{28,4},{1,9},{5... | collective-permute-start | bytes 786440 | tf_op jit(solution)/shard_map/ppermute | solution.py:667
  14.6 3.5 %collective-permute-done.refs_4_.refs_14_ = bf16[512,256]{1,0:T(8,128)(2,1)S(1)} collective-permute-done((bf16[512,256]{1,0:T(8,128)(2,1)}, bf16[512,256]{1,0:T(8,128)(2,1)S(1)}, u32[]{:S(2)}, u32[]{:S(2)}) %collective-permute-start) | collective-permute-done | bytes 262176 | tf_op jit(solution)/shard_map/ppermute | solution.py:667
  19.9 8.6 %collective-permute-done.1.refs_5_.refs_15_ = bf16[512,256]{1,0:T(8,128)(2,1)S(1)} collective-permute-done((bf16[512,256]{1,0:T(8,128)(2,1)}, bf16[512,256]{1,0:T(8,128)(2,1)S(1)}, u32[]{:S(2)}, u32[]{:S(2)}) %collective-permute-start.1) | collective-permute-done | bytes 262176 | tf_op jit(solution)/shard_map/ppermute | solution.py:667
  34.3 7.8 %shard_map.283 = (f32[2,1024,256]{2,1,0:T(8,128)}, bf16[2,1024,128]{2,1,0:T(8,128)(2,1)}) custom-call(s32[16]{0:T(128)} %refs_0_.11, s32[4]{0:T(128)} %get-tuple-element.57.refs_1_, bf16[512,256]{1,0:T(8,128)(2,1)} %get-tuple-element.58.refs_2_, bf16[512,256]{1,0:T(8,128)(2,1)} %get-tuple-element.59.refs_3_.refs_13_, bf16[512,256]{1,0:T(8,128)(2,1)} %copy-done.19, ...), custom_call_target="tpu_custom_call" | custom-call | flops 1000 | tf_op jit(solution)/shard_map/pallas_call | solution.py:638
  43.1 6.5 %shard_map.284 = (bf16[512,256]{1,0:T(8,128)(2,1)}, f32[512,256]{1,0:T(8,128)}, f32[2,8,1024]{2,1,0:T(8,128)}, bf16[256,1024]{1,0:T(8,128)(2,1)}, bf16[256,1024]{1,0:T(8,128)(2,1)}) custom-call(s32[16]{0:T(128)} %refs_0_.11, s32[4]{0:T(128)} %get-tuple-element.57.refs_1_, bf16[2,1024,128]{2,1,0:T(8,128)(2,1)} %get-tuple-element.60.refs_2_, ...), custom_call_target="tpu_custom_call" | custom-call | flops 1000 | tf_op jit(solution)/shard_map/pallas_call | solution.py:638
  54.5 12.5 %collective-permute-done.8 = bf16[256,1024]{1,0:T(8,128)(2,1)S(1)} collective-permute-done((bf16[256,1024]{1,0:T(8,128)(2,1)S(1)}, bf16[256,1024]{1,0:T(8,128)(2,1)S(1)}, u32[]{:S(2)}, u32[]{:S(2)}) %collective-permute-start.8) | collective-permute-done | bytes 524320 | tf_op jit(solution)/shard_map/ppermute | solution.py:662
  70.0 11.0 %shard_map.285 = (f32[512,1024]{1,0:T(8,128)}, bf16[512,1024]{1,0:T(8,128)(2,1)}, bf16[512,1152]{1,0:T(8,128)(2,1)}, bf16[512,1152]{1,0:T(8,128)(2,1)}, bf16[512...) custom-call(bf16[512,1024]{1,0:T(8,128)(2,1)} %get-tuple-element.56.refs_0_.refs_9_, ...), custom_call_target="tpu_custom_call" | custom-call | flops 1000 | tf_op jit(solution)/shard_map/pallas_call | solution.py:638
  86.0 11.9 %shard_map.286 = (bf16[256,1024]{1,0:T(8,128)(2,1)}, bf16[256,1024]{1,0:T(8,128)(2,1)}, bf16[4,128,896]{2,1,0:T(8,128)(2,1)}, bf16[4,128,896]{2,1,0:T(8,128)(2,1...) custom-call(bf16[512,1024]{1,0:T(8,128)(2,1)} %copy-done.8, ...), custom_call_target="tpu_custom_call" | custom-call | flops 14000000000 | tf_op jit(solution)/shard_map/pallas_call | solution.py:579
  97.9 10.1 %collective-permute-start.16 = (bf16[4,128,1792]{2,1,0:T(8,128)(2,1)}, bf16[4,128,1792]{2,1,0:T(8,128)(2,1)S(1)}, u32[]{:S(2)}, u32[]{:S(2)}) collective-permute-start(bf16[4,128,1792]{2,1,0:T(8,128)(2,1)} %get-tuple-element.89), channel_id=1, source_target_pairs={{0,8},{4,12},{8,0},{12,4},{16,24},{20,28},{24,16},{28,20},{1,9},{5... | collective-permute-start | bytes 5505032 | tf_op jit(solution)/shard_map/ppermute | solution.py:662
  111.8 11.7 %shard_map.288 = (bf16[4,512,256]{2,1,0:T(8,128)(2,1)}, f32[2,128,1024]{2,1,0:T(8,128)}, f32[512,1024]{1,0:T(8,128)}, bf16[512,1024]{1,0:T(8,128)(2,1)}, bf16[512,256]{1,0:T(8,128)(2,1)}, /*index=5*/f32[1,1024]{1,0:T(1,128)}) custom-call(s32[16]{0:T(128)} %refs_0_.11, s32[4]{0:T(128)} %get-tuple-element.57.refs_1_, ...), custom_call_target="tpu_custom_call" | custom-call | flops 1000 | tf_op jit(solution)/shard_map/pallas_call | solution.py:638
  126.3 9.8 %shard_map.289 = (bf16[4,512,256]{2,1,0:T(8,128)(2,1)}, bf16[512,256]{1,0:T(8,128)(2,1)}, f32[1,128]{1,0:T(1,128)}) custom-call(s32[16]{0:T(128)} %refs_0_.11, s32[4]{0:T(128)} %get-tuple-element.57.refs_1_, bf16[512,256]{1,0:T(8,128)(2,1)} %get-tuple-element.58.refs_2_, bf16[512,256]{1,0:T(8,128)(2,1)} %get-tuple-element.76.refs_3_, ...), custom_call_target="tpu_custom_call" | custom-call | flops 1000 | tf_op jit(solution)/shard_map/pallas_call | solution.py:638
  138.6 5.4 %collective-permute-start.20 = (bf16[2,128,896]{2,1,0:T(8,128)(2,1)S(1)}, bf16[2,128,896]{2,1,0:T(8,128)(2,1)}, u32[]{:S(2)}, u32[]{:S(2)}) collective-permute-start(bf16[2,128,896]{2,1,0:T(8,128)(2,1)S(1)} %get-tuple-element.138.refs_6_), channel_id=1, source_target_pairs={{0,8},{4,12},{8,0},{12,4},{16,24},{20,28},{24,16},{28,20},{1,9},{5... | collective-permute-start | bytes 1376264 | tf_op jit(solution)/shard_map/ppermute | solution.py:662
  144.0 8.6 %shard_map.291 = (bf16[4,128,1280]{2,1,0:T(8,128)(2,1)}, bf16[4,128,1280]{2,1,0:T(8,128)(2,1)}) custom-call(bf16[512,1024]{1,0:T(8,128)(2,1)} %get-tuple-element.65.n2_ref.refs_0_, bf16[512,1152]{1,0:T(8,128)(2,1)} %get-tuple-element.67.dgate_ref.refs_1_, bf16[512,1024]{1,0:T(8,128)(2,1)} %get-tuple-element.83.refs_2_.refs_0_, ...), custom_call_target="tpu_custom_call" | custom-call | flops 1000 | tf_op jit(solution)/shard_map/pallas_call | solution.py:638
  152.6 3.2 %fusion.1 = (bf16[2,128,1792]{2,1,0:T(8,128)(2,1)}, bf16[2,128,1792]{2,1,0:T(8,128)(2,1)}) fusion(bf16[2,2,1,128,1792]{4,3,1,0,2:T(8,128)(2,1)S(1)} %bitcast.107, s32[]{:T(128)S(6)} %select_n.148, bf16[2,2,1,128,1792]{4,3,1,0,2:T(8,128)(2,1)} %bitcast.104, s32[]{:T(128)S(6)} %select_n.142), kind=kLoop, calls=%fused_computation.19 | loop fusion | flops 3670016 | bytes 5505032 | tf_op jit(solution)/shard_map/convert_element_type | solution.py:695
  163.4 14.1 %collective-permute-done.18 = bf16[2,512,256]{2,1,0:T(8,128)(2,1)} collective-permute-done((bf16[2,512,256]{2,1,0:T(8,128)(2,1)S(1)}, bf16[2,512,256]{2,1,0:T(8,128)(2,1)}, u32[]{:S(2)}, u32[]{:S(2)}) %collective-permute-start.18) | collective-permute-done | bytes 524320 | tf_op jit(solution)/shard_map/ppermute | solution.py:662
  183.8 8.2 %collective-permute-done.19 = bf16[1,512,256]{2,1,0:T(8,128)(2,1)S(1)} collective-permute-done((bf16[1,512,256]{2,1,0:T(8,128)(2,1)S(1)}, bf16[1,512,256]{2,1,0:T(8,128)(2,1)S(1)}, u32[]{:S(2)}, u32[]{:S(2)}) %collective-permute-start.19) | collective-permute-done | bytes 262176 | tf_op jit(solution)/shard_map/ppermute | solution.py:662
  192.7 4.6 %shard_map.296 = (bf16[512,256]{1,0:T(8,128)(2,1)}, bf16[256,1024]{1,0:T(8,128)(2,1)}, bf16[256,1024]{1,0:T(8,128)(2,1)}, f32[1,2304]{1,0:T(1,128)}) custom-call(s32[16]{0:T(128)} %refs_0_.11, s32[4]{0:T(128)} %get-tuple-element.57.refs_1_, f32[512,384]{1,0:T(8,128)} %get-tuple-element.73.refs_6_.refs_2_, f32[1,64]{1,0:T(1,128)} %bitcast.120, ...), custom_call_target="tpu_custom_call" | custom-call | flops 1000 | tf_op jit(solution)/shard_map/pallas_call | solution.py:638
  201.7 3.4 %shard_map.297 = (bf16[4,144,256]{2,1,0:T(8,128)(2,1)}, bf16[4,144,256]{2,1,0:T(8,128)(2,1)}) custom-call(bf16[512,1024]{1,0:T(8,128)(2,1)} %get-tuple-element.83.refs_2_.refs_0_, bf16[512,256]{1,0:T(8,128)(2,1)} %get-tuple-element.94.refs_1_, f32[1,2304]{1,0:T(1,128)} %get-tuple-element.95.refs_2_, bf16[256,1024]{1,0:T(8,128)(2,1)} %copy-done), custom_call_target="tpu_custom_call" | custom-call | flops 1000 | tf_op jit(solution)/shard_map/pallas_call | solution.py:638
  207.2 3.0 %fusion.3 = (bf16[2,128,1280]{2,1,0:T(8,128)(2,1)}, bf16[2,128,1280]{2,1,0:T(8,128)(2,1)}) fusion(bf16[2,2,1,128,1280]{4,3,1,0,2:T(8,128)(2,1)} %bitcast.25, s32[]{:T(128)S(6)} %select_n.143, bf16[2,2,1,128,1280]{4,3,1,0,2:T(8,128)(2,1)} %bitcast.105, s32[]{:T(128)S(6)} %select_n.140), kind=kLoop, calls=%fused_computation.26 | loop fusion | flops 2621440 | bytes 3932168 | tf_op jit(solution)/shard_map/convert_element_type | solution.py:695
  211.3 3.4 %collective-permute-done.25 = bf16[256,1024]{1,0:T(8,128)(2,1)S(1)} collective-permute-done((bf16[256,1024]{1,0:T(8,128)(2,1)S(1)}, bf16[256,1024]{1,0:T(8,128)(2,1)S(1)}, u32[]{:S(2)}, u32[]{:S(2)}) %collective-permute-start.25) | collective-permute-done | bytes 524320 | tf_op jit(solution)/shard_map/ppermute | solution.py:662
  222.0 4.5 %shard_map.303.refs_1_ = f32[512,1024]{1,0:T(8,128)} custom-call(bf16[512,1024]{1,0:T(8,128)(2,1)} %get-tuple-element.56.refs_0_.refs_9_, bf16[256,1024]{1,0:T(8,128)(2,1)} %copy-done.4, bf16[256,1024]{1,0:T(8,128)(2,1)} %collective-permute-done.27.refs_2_, f32[1,1024]{1,0:T(1,128)} %bitcast.116, f32[512,1024]{1,0:T(8,128)} %get-tuple-element.97.refs_4_, ...), custom_call_target="tpu_custom_call" | custom-call | flops 1000 | tf_op jit(solution)/shard_map/pallas_call | solution.py:638
  226.5 11.0 %collective-permute-done.29 = bf16[2,128,1280]{2,1,0:T(8,128)(2,1)} collective-permute-done((bf16[2,128,1280]{2,1,0:T(8,128)(2,1)}, bf16[2,128,1280]{2,1,0:T(8,128)(2,1)}, u32[]{:S(2)}, u32[]{:S(2)}) %collective-permute-start.29) | collective-permute-done | bytes 655392 | tf_op jit(solution)/shard_map/ppermute | solution.py:662
  246.9 6.5 %collective-permute-done.32 = bf16[1,144,256]{2,1,0:T(8,128)(2,1)S(1)} collective-permute-done((bf16[1,144,256]{2,1,0:T(8,128)(2,1)S(1)}, bf16[1,144,256]{2,1,0:T(8,128)(2,1)S(1)}, u32[]{:S(2)}, u32[]{:S(2)}) %collective-permute-start.32) | collective-permute-done | bytes 73760 | tf_op jit(solution)/shard_map/ppermute | solution.py:662
  (190 shorter events, 84.8 us)
Async XLA Ops:
  8.6 19.9 %collective-permute-start.1 = (bf16[512,256]{1,0:T(8,128)(2,1)}, bf16[512,256]{1,0:T(8,128)(2,1)S(1)}, u32[]{:S(2)}, u32[]{:S(2)}) collective-permute-start(bf16[512,256]{1,0:T(8,128)(2,1)} %get-tuple-element.59.refs_3_.refs_13_), channel_id=1, source_target_pairs={{0,16},{4,20},{8,24},{12,28},{16,0},{20,4},{24,8},{28,12},{1,17},{... | collective-permute-start | bytes 786440 | tf_op jit(solution)/shard_map/ppermute | solution.py:667
  11.2 18.8 %collective-permute-start.2 = (bf16[512,256]{1,0:T(8,128)(2,1)}, bf16[512,256]{1,0:T(8,128)(2,1)S(1)}, u32[]{:S(2)}, u32[]{:S(2)}) collective-permute-start(bf16[512,256]{1,0:T(8,128)(2,1)} %get-tuple-element.59.refs_3_.refs_13_), channel_id=1, source_target_pairs={{0,24},{4,28},{8,0},{12,4},{16,8},{20,12},{24,16},{28,20},{1,25},{... | collective-permute-start | bytes 786440 | tf_op jit(solution)/shard_map/ppermute | solution.py:667
  12.6 21.0 %collective-permute-start.3 = (bf16[512,256]{1,0:T(8,128)(2,1)}, bf16[512,256]{1,0:T(8,128)(2,1)S(1)}, u32[]{:S(2)}, u32[]{:S(2)}) collective-permute-start(bf16[512,256]{1,0:T(8,128)(2,1)} %get-tuple-element.59.refs_3_.refs_13_), channel_id=1, source_target_pairs={{0,4},{4,0},{8,12},{12,8},{16,20},{20,16},{24,28},{28,24},{1,5},{5... | collective-permute-start | bytes 786440 | tf_op jit(solution)/shard_map/ppermute | solution.py:662
  18.1 24.0 %collective-permute-start.4 = (bf16[512,256]{1,0:T(8,128)(2,1)S(1)}, bf16[512,256]{1,0:T(8,128)(2,1)S(1)}, u32[]{:S(2)}, u32[]{:S(2)}) collective-permute-start(bf16[512,256]{1,0:T(8,128)(2,1)S(1)} %collective-permute-done.refs_4_.refs_14_), channel_id=1, source_target_pairs={{0,4},{4,0},{8,12},{12,8},{16,20},{20,16},{24,28},{28,24},{1,5},{5... | collective-permute-start | bytes 786440 | tf_op jit(solution)/shard_map/ppermute | solution.py:662
  28.5 13.6 %collective-permute-start.5 = (bf16[512,256]{1,0:T(8,128)(2,1)S(1)}, bf16[512,256]{1,0:T(8,128)(2,1)S(1)}, u32[]{:S(2)}, u32[]{:S(2)}) collective-permute-start(bf16[512,256]{1,0:T(8,128)(2,1)S(1)} %collective-permute-done.1.refs_5_.refs_15_), channel_id=1, source_target_pairs={{0,4},{4,0},{8,12},{12,8},{16,20},{20,16},{24,28},{28,24},{1,5},{5... | collective-permute-start | bytes 786440 | tf_op jit(solution)/shard_map/ppermute | solution.py:662
  53.0 14.0 %collective-permute-start.8 = (bf16[256,1024]{1,0:T(8,128)(2,1)S(1)}, bf16[256,1024]{1,0:T(8,128)(2,1)S(1)}, u32[]{:S(2)}, u32[]{:S(2)}) collective-permute-start(bf16[256,1024]{1,0:T(8,128)(2,1)S(1)} %add_convert_fusion.15), channel_id=1, source_target_pairs={{0,2},{1,3},{2,0},{3,1},{4,6},{5,7},{6,4},{7,5},{8,10},{9,11},{10,... | collective-permute-start | bytes 1572872 | tf_op jit(solution)/shard_map/ppermute | solution.py:662
  84.4 23.6 %collective-permute-start.12 = (bf16[256,1024]{1,0:T(8,128)(2,1)S(1)}, bf16[256,1024]{1,0:T(8,128)(2,1)S(1)}, u32[]{:S(2)}, u32[]{:S(2)}) collective-permute-start(bf16[256,1024]{1,0:T(8,128)(2,1)S(1)} %add_convert_fusion.13.refs_0_), channel_id=1, source_target_pairs={{0,2},{1,3},{2,0},{3,1},{4,6},{5,7},{6,4},{7,5},{8,10},{9,11},{10,... | collective-permute-start | bytes 1572872 | tf_op jit(solution)/shard_map/ppermute | solution.py:662
  97.9 54.7 %collective-permute-start.16 = (bf16[4,128,1792]{2,1,0:T(8,128)(2,1)}, bf16[4,128,1792]{2,1,0:T(8,128)(2,1)S(1)}, u32[]{:S(2)}, u32[]{:S(2)}) collective-permute-start(bf16[4,128,1792]{2,1,0:T(8,128)(2,1)} %get-tuple-element.89), channel_id=1, source_target_pairs={{0,8},{4,12},{8,0},{12,4},{16,24},{20,28},{24,16},{28,20},{1,9},{5... | collective-permute-start | bytes 5505032 | tf_op jit(solution)/shard_map/ppermute | solution.py:662
  109.8 26.3 %collective-permute-start.15 = (bf16[4,128,896]{2,1,0:T(8,128)(2,1)}, bf16[4,128,896]{2,1,0:T(8,128)(2,1)}, u32[]{:S(2)}, u32[]{:S(2)}) collective-permute-start(bf16[4,128,896]{2,1,0:T(8,128)(2,1)} %get-tuple-element.87), channel_id=1, source_target_pairs={{0,4},{4,0},{8,12},{12,8},{16,20},{20,16},{24,28},{28,24},{1,5},{5... | collective-permute-start | bytes 2752520 | tf_op jit(solution)/shard_map/ppermute | solution.py:662
  111.1 14.2 %collective-permute-start.13 = (bf16[256,1024]{1,0:T(8,128)(2,1)}, bf16[256,1024]{1,0:T(8,128)(2,1)S(1)}, u32[]{:S(2)}, u32[]{:S(2)}) collective-permute-start(bf16[256,1024]{1,0:T(8,128)(2,1)} %shard_map.287.refs_15_), channel_id=1, source_target_pairs={{0,2},{1,3},{2,0},{3,1},{4,6},{5,7},{6,4},{7,5},{8,10},{9,11},{10,... | collective-permute-start | bytes 1572872 | tf_op jit(solution)/shard_map/ppermute | solution.py:662
  123.5 33.4 %collective-permute-start.17 = (bf16[4,512,256]{2,1,0:T(8,128)(2,1)}, bf16[4,512,256]{2,1,0:T(8,128)(2,1)}, u32[]{:S(2)}, u32[]{:S(2)}) collective-permute-start(bf16[4,512,256]{2,1,0:T(8,128)(2,1)} %get-tuple-element.90), channel_id=1, source_target_pairs={{0,4},{4,0},{8,12},{12,8},{16,20},{20,16},{24,28},{28,24},{1,5},{5... | collective-permute-start | bytes 3145736 | tf_op jit(solution)/shard_map/ppermute | solution.py:662
  138.6 21.0 %collective-permute-start.20 = (bf16[2,128,896]{2,1,0:T(8,128)(2,1)S(1)}, bf16[2,128,896]{2,1,0:T(8,128)(2,1)}, u32[]{:S(2)}, u32[]{:S(2)}) collective-permute-start(bf16[2,128,896]{2,1,0:T(8,128)(2,1)S(1)} %get-tuple-element.138.refs_6_), channel_id=1, source_target_pairs={{0,8},{4,12},{8,0},{12,4},{16,24},{20,28},{24,16},{28,20},{1,9},{5... | collective-permute-start | bytes 1376264 | tf_op jit(solution)/shard_map/ppermute | solution.py:662
  156.9 24.5 %collective-permute-start.22 = (bf16[2,128,1792]{2,1,0:T(8,128)(2,1)S(1)}, bf16[2,128,1792]{2,1,0:T(8,128)(2,1)S(1)}, u32[]{:S(2)}, u32[]{:S(2)}) collective-permute-start(bf16[2,128,1792]{2,1,0:T(8,128)(2,1)S(1)} %copy-done.13), channel_id=1, source_target_pairs={{0,4},{4,0},{8,12},{12,8},{16,20},{20,16},{24,28},{28,24},{1,5},{5... | collective-permute-start | bytes 2752520 | tf_op jit(solution)/shard_map/ppermute | solution.py:662
  158.7 18.8 %collective-permute-start.18 = (bf16[2,512,256]{2,1,0:T(8,128)(2,1)S(1)}, bf16[2,512,256]{2,1,0:T(8,128)(2,1)}, u32[]{:S(2)}, u32[]{:S(2)}) collective-permute-start(bf16[2,512,256]{2,1,0:T(8,128)(2,1)S(1)} %get-tuple-element.134.refs_1_), channel_id=1, source_target_pairs={{0,8},{4,12},{8,0},{12,4},{16,24},{20,28},{24,16},{28,20},{1,9},{5... | collective-permute-start | bytes 1572872 | tf_op jit(solution)/shard_map/ppermute | solution.py:662
  161.4 18.0 %collective-permute-start.21 = (bf16[1,128,896]{2,1,0:T(8,128)(2,1)}, bf16[1,128,896]{2,1,0:T(8,128)(2,1)}, u32[]{:S(2)}, u32[]{:S(2)}) collective-permute-start(bf16[1,128,896]{2,1,0:T(8,128)(2,1)} %add_convert_fusion.22), channel_id=1, source_target_pairs={{0,16},{4,20},{8,24},{12,28},{16,0},{20,4},{24,8},{28,12},{1,17},{... | collective-permute-start | bytes 688136 | tf_op jit(solution)/shard_map/ppermute | solution.py:662
  161.4 45.9 %collective-permute-start.24 = (bf16[4,128,1280]{2,1,0:T(8,128)(2,1)}, bf16[4,128,1280]{2,1,0:T(8,128)(2,1)}, u32[]{:S(2)}, u32[]{:S(2)}) collective-permute-start(bf16[4,128,1280]{2,1,0:T(8,128)(2,1)} %shard_map.299), channel_id=1, source_target_pairs={{0,4},{4,0},{8,12},{12,8},{16,20},{20,16},{24,28},{28,24},{1,5},{5... | collective-permute-start | bytes 3932168 | tf_op jit(solution)/shard_map/ppermute | solution.py:662
  179.4 12.6 %collective-permute-start.19 = (bf16[1,512,256]{2,1,0:T(8,128)(2,1)S(1)}, bf16[1,512,256]{2,1,0:T(8,128)(2,1)S(1)}, u32[]{:S(2)}, u32[]{:S(2)}) collective-permute-start(bf16[1,512,256]{2,1,0:T(8,128)(2,1)S(1)} %get-tuple-element.139.refs_1_), channel_id=1, source_target_pairs={{0,16},{4,20},{8,24},{12,28},{16,0},{20,4},{24,8},{28,12},{1,17},{... | collective-permute-start | bytes 786440 | tf_op jit(solution)/shard_map/ppermute | solution.py:662
  200.7 14.0 %collective-permute-start.25 = (bf16[256,1024]{1,0:T(8,128)(2,1)S(1)}, bf16[256,1024]{1,0:T(8,128)(2,1)S(1)}, u32[]{:S(2)}, u32[]{:S(2)}) collective-permute-start(bf16[256,1024]{1,0:T(8,128)(2,1)S(1)} %add_convert_fusion.7.refs_3_.refs_0_), channel_id=1, source_target_pairs={{0,2},{1,3},{2,0},{3,1},{4,6},{5,7},{6,4},{7,5},{8,10},{9,11},{10,... | collective-permute-start | bytes 1572872 | tf_op jit(solution)/shard_map/ppermute | solution.py:662
  201.7 17.7 %collective-permute-start.26 = (bf16[256,1024]{1,0:T(8,128)(2,1)S(1)}, bf16[256,1024]{1,0:T(8,128)(2,1)}, u32[]{:S(2)}, u32[]{:S(2)}) collective-permute-start(bf16[256,1024]{1,0:T(8,128)(2,1)S(1)} %copy-done.3), channel_id=1, source_target_pairs={{0,1},{1,0},{2,3},{3,2},{4,5},{5,4},{6,7},{7,6},{8,9},{9,8},{10,11... | collective-permute-start | bytes 1572872 | tf_op jit(solution)/shard_map/ppermute | solution.py:662
  201.7 39.4 %collective-permute-start.33 = (bf16[1,128,1792]{2,1,0:T(8,128)(2,1)}, bf16[1,128,1792]{2,1,0:T(8,128)(2,1)}, u32[]{:S(2)}, u32[]{:S(2)}) collective-permute-start(bf16[1,128,1792]{2,1,0:T(8,128)(2,1)} %get-tuple-element.136.refs_18_), channel_id=1, source_target_pairs={{0,16},{4,20},{8,24},{12,28},{16,0},{20,4},{24,8},{28,12},{1,17},{... | collective-permute-start | bytes 1376264 | tf_op jit(solution)/shard_map/ppermute | solution.py:662
  210.3 27.2 %collective-permute-start.29 = (bf16[2,128,1280]{2,1,0:T(8,128)(2,1)}, bf16[2,128,1280]{2,1,0:T(8,128)(2,1)}, u32[]{:S(2)}, u32[]{:S(2)}) collective-permute-start(bf16[2,128,1280]{2,1,0:T(8,128)(2,1)} %get-tuple-element.132.refs_1_), channel_id=1, source_target_pairs={{0,8},{4,12},{8,0},{12,4},{16,24},{20,28},{24,16},{28,20},{1,9},{5... | collective-permute-start | bytes 1966088 | tf_op jit(solution)/shard_map/ppermute | solution.py:662
  219.3 20.2 %collective-permute-start.31 = (bf16[2,144,256]{2,1,0:T(8,128)(2,1)S(1)}, bf16[2,144,256]{2,1,0:T(8,128)(2,1)S(1)}, u32[]{:S(2)}, u32[]{:S(2)}) collective-permute-start(bf16[2,144,256]{2,1,0:T(8,128)(2,1)S(1)} %get-tuple-element.146.refs_5_), channel_id=1, source_target_pairs={{0,8},{4,12},{8,0},{12,4},{16,24},{20,28},{24,16},{28,20},{1,9},{5... | collective-permute-start | bytes 442376 | tf_op jit(solution)/shard_map/ppermute | solution.py:662
  240.4 12.9 %collective-permute-start.32 = (bf16[1,144,256]{2,1,0:T(8,128)(2,1)S(1)}, bf16[1,144,256]{2,1,0:T(8,128)(2,1)S(1)}, u32[]{:S(2)}, u32[]{:S(2)}) collective-permute-start(bf16[1,144,256]{2,1,0:T(8,128)(2,1)S(1)} %add_convert_fusion.26.refs_1_), channel_id=1, source_target_pairs={{0,16},{4,20},{8,24},{12,28},{16,0},{20,4},{24,8},{28,12},{1,17},{... | collective-permute-start | bytes 221192 | tf_op jit(solution)/shard_map/ppermute | solution.py:662
  242.5 17.3 %collective-permute-start.30 = (bf16[1,128,1280]{2,1,0:T(8,128)(2,1)S(1)}, bf16[1,128,1280]{2,1,0:T(8,128)(2,1)S(1)}, u32[]{:S(2)}, u32[]{:S(2)}) collective-permute-start(bf16[1,128,1280]{2,1,0:T(8,128)(2,1)S(1)} %copy-done.18), channel_id=1, source_target_pairs={{0,16},{4,20},{8,24},{12,28},{16,0},{20,4},{24,8},{28,12},{1,17},{... | collective-permute-start | bytes 983048 | tf_op jit(solution)/shard_map/ppermute | solution.py:662
  (48 other events, 264.9 us)
